TPU v7x, 256 devices: a whole 4x4x8 slice. The times are simulated.
256 devices in a mesh: dp: 16 (over z, y_hi), tensor: 16 (over y_lo, x, core).
Axes of the slice: x: 4, y: 4 (y_hi: 2, y_lo: 2; y = y_hi * 2 + y_lo), z: 8, core: 2. Of those that a mesh axis runs over, the one named last changes fastest.
Arguments:
- tokens: bfloat16 [8192, 4608], P(('dp', 'tensor')), may hold values from -0.7 to 0.7
- norm_gain: float32 [4608], replicated, may hold values from 0.5 to 1.5
- w_query: bfloat16 [4608, 4096], P(None, 'tensor'), may hold values from -0.073656956 to 0.073656956
- w_key: bfloat16 [4608, 2048], P(None, 'tensor'), may hold values from -0.073656956 to 0.073656956
- w_value: bfloat16 [4608, 2048], P(None, 'tensor'), may hold values from -0.09375 to 0.09375
- w_output: bfloat16 [4096, 4608], P('tensor'), may hold values from -0.09375 to 0.09375
- d_mixed: bfloat16 [8192, 4608], P(('dp', 'tensor')), may hold values from -24 to 24
Outputs:
- mixed: bfloat16 [8192, 4608], P(('dp', 'tensor'))
- d_tokens: bfloat16 [8192, 4608], P(('dp', 'tensor'))
- dw_query: float32 [4608, 4096], P('dp', 'tensor')
- dw_key: float32 [4608, 2048], P('dp', 'tensor')
- dw_value: float32 [4608, 2048], P('dp', 'tensor')
- dw_output: float32 [4096, 4608], P('tensor', 'dp')
All inputs are finite; a program needn't handle non-finite values.
Results may differ from a plain program's by a relative error of at most 0.025.
Values may be sent and summed in bfloat16 or wider, within the bound.
A program may use at most 128 MiB of HBM per device.

v0:
```python
import math

import jax
import jax.numpy as jnp
from jax import lax
from jax.sharding import PartitionSpec as P

D = 4608
HEADS = 32
HEAD = 128


cap_value = 50.0


def norm_rows(tokens, norm_gain):
    values = tokens.astype(jnp.float32)
    scale = lax.rsqrt(jnp.mean(values * values, axis=-1, keepdims=True) + 1e-06)
    return (values * scale * norm_gain).astype(jnp.bfloat16)


def attend(query, key, value):
    length = query.shape[0]
    groups = key.shape[1] // HEAD
    ratio = query.shape[1] // key.shape[1]
    qf = query.astype(jnp.float32).reshape(length, groups, ratio, HEAD)
    kf = key.astype(jnp.float32).reshape(length, groups, HEAD)
    vf = value.astype(jnp.float32).reshape(length, groups, HEAD)
    scores = jnp.einsum("skgd,tkd->kgst", qf, kf) / math.sqrt(D // HEADS)
    capped = cap_value * jnp.tanh(scores / cap_value)
    row_pos = lax.broadcasted_iota(jnp.int32, (length, length), 0)
    col_pos = lax.broadcasted_iota(jnp.int32, (length, length), 1)
    visible = row_pos >= col_pos
    weights = jnp.where(visible, jnp.exp(capped), 0.0)
    log_total = jnp.log(jnp.sum(weights, axis=-1, keepdims=True))
    probs = jnp.exp(jnp.where(visible, capped - log_total, -1e30)).astype(jnp.bfloat16)
    context = jnp.einsum("kgst,tkd->skgd", probs.astype(jnp.float32), vf)
    return context.reshape(length, groups * ratio * HEAD).astype(jnp.bfloat16)


def inner_rows(left, right):
    return lax.dot_general(
        left, right, (((0,), (0,)), ((), ())), preferred_element_type=jnp.float32
    )


def right_trans(left, right):
    return lax.dot_general(
        left, right, (((1,), (1,)), ((), ())), preferred_element_type=jnp.float32
    )


def on_device(tokens, norm_gain, w_query, w_key, w_value, w_output, d_mixed):
    normed = lax.all_gather(norm_rows(tokens, norm_gain), "tensor", axis=0, tiled=True)
    query = jnp.dot(normed, w_query, preferred_element_type=jnp.float32).astype(jnp.bfloat16)
    key = jnp.dot(normed, w_key, preferred_element_type=jnp.float32).astype(jnp.bfloat16)
    value = jnp.dot(normed, w_value, preferred_element_type=jnp.float32).astype(jnp.bfloat16)
    context, back = jax.vjp(attend, query, key, value)
    summed = lax.psum_scatter(
        jnp.dot(context, w_output, preferred_element_type=jnp.float32).astype(jnp.bfloat16),
        "tensor",
        scatter_dimension=0,
        tiled=True,
    ).astype(jnp.float32)
    mixed = (tokens.astype(jnp.float32) + summed).astype(jnp.bfloat16)
    cotangent = lax.all_gather(d_mixed, "tensor", axis=0, tiled=True)
    d_context = right_trans(cotangent, w_output).astype(jnp.bfloat16)
    d_query, d_key, d_value = back(d_context)
    term = right_trans(d_query, w_query)
    term = term + right_trans(d_key, w_key)
    d_normed = lax.psum_scatter(
        (term + right_trans(d_value, w_value)).astype(jnp.bfloat16),
        "tensor",
        scatter_dimension=0,
        tiled=True,
    ).astype(jnp.float32)
    values = tokens.astype(jnp.float32)
    scale = lax.rsqrt(jnp.mean(values * values, axis=-1, keepdims=True) + 1e-06)
    upstream = norm_gain * d_normed
    back_norm = scale * upstream - values * scale**3 * jnp.mean(
        upstream * values, axis=-1, keepdims=True
    )
    d_tokens = (d_mixed.astype(jnp.float32) + back_norm).astype(jnp.bfloat16)
    dw_query, dw_key, dw_value, dw_out_t = (
        lax.psum_scatter(
            inner_rows(normed, d_query).astype(jnp.bfloat16), "dp", scatter_dimension=0, tiled=True
        ).astype(jnp.float32),
        lax.psum_scatter(
            inner_rows(normed, d_key).astype(jnp.bfloat16), "dp", scatter_dimension=0, tiled=True
        ).astype(jnp.float32),
        lax.psum_scatter(
            inner_rows(normed, d_value).astype(jnp.bfloat16), "dp", scatter_dimension=0, tiled=True
        ).astype(jnp.float32),
        lax.psum_scatter(
            inner_rows(cotangent, context).astype(jnp.bfloat16),
            "dp",
            scatter_dimension=0,
            tiled=True,
        ).astype(jnp.float32),
    )
    return (mixed, d_tokens, dw_query, dw_key, dw_value, dw_out_t.T)


def solution(mesh):
    return jax.shard_map(
        on_device,
        mesh=mesh,
        in_specs=(
            P(("dp", "tensor"), None),
            P(),
            P(None, "tensor"),
            P(None, "tensor"),
            P(None, "tensor"),
            P("tensor", None),
            P(("dp", "tensor"), None),
        ),
        out_specs=(
            P(("dp", "tensor"), None),
            P(("dp", "tensor"), None),
            P("dp", "tensor"),
            P("dp", "tensor"),
            P("dp", "tensor"),
            P("tensor", "dp"),
        ),
        check_vma=False,
    )
```

profile of v0, /device:TPU:1, one launch (start us, length us, event | category | flops | bytes accessed | tf_op | source)
XLA Modules:
  0.0 1094.6 jit_solution(2296280454182097670)
XLA Ops:
  7.2 0.0 copy-start
  7.2 0.0 all-gather.3.cloned.1.call-start
  7.2 1.3 fusion.15
  8.5 1.8 fusion.17
  10.3 0.0 all-gather.3.cloned.1.call-update
  10.4 0.0 all-gather.5.cloned.1.call-start
  10.4 0.7 all-gather.5.cloned.1.call-update
  11.1 0.0 reduce-scatter.15.cloned.1.call-start
  11.2 0.1 iota_compare_fusion
  11.3 0.0 copy-start.7
  11.3 44.4 %all-gather.3.cloned.1.call-done = bf16[512,4608]{1,0:T(8,128)(2,1)} async-done(((bf16[32,4608]{1,0:T(8,128)(2,1)}), bf16[512,4608]{1,0:T(8,128)(2,1)}) %all-gather.3.cloned.1.call-update) | async-done | bytes 4718608 | tf_op jit(solution)/shard_map/all_gather | solution.py:54
  55.7 4.2 fusion.13
  59.9 0.0 copy-start.16
  59.9 1.4 convolution_convert_fusion.9
  61.4 0.0 copy-start.4
  61.4 2.1 select_reduce_fusion
  63.6 1.4 fusion.12
  64.9 0.0 copy-start.18
  65.0 33.6 %all-gather.5.cloned.1.call-done = bf16[512,4608]{1,0:T(8,128)(2,1)} async-done(((bf16[32,4608]{1,0:T(8,128)(2,1)}), bf16[512,4608]{1,0:T(8,128)(2,1)}) %all-gather.5.cloned.1.call-update) | async-done | bytes 4718608 | tf_op jit(solution)/shard_map/all_gather | solution.py:66
  98.5 4.6 convolution_convert_fusion.7
  103.2 0.0 copy-start.17
  103.2 0.9 fusion.7
  104.2 2.4 fusion.2
  106.6 0.4 fusion.10
  107.0 2.5 convolution_convert_fusion.4
  109.5 0.0 reduce-scatter.15.cloned.1.call-update
  109.5 0.0 reduce-scatter.17.cloned.1.call-start
  109.6 2.4 fusion.11
  112.0 0.6 copy-done.10
  112.6 4.8 convolution_convert_fusion.3
  117.4 0.0 reduce-scatter.17.cloned.1.call-update
  117.5 0.2 reduce-scatter.19.cloned.1.call-start
  117.7 2.3 convolution_convert_fusion.8
  120.1 0.7 copy-done.12
  120.8 5.2 fusion
  125.9 4.3 copy.35
  130.2 0.0 reduce-scatter.19.cloned.1.call-update
  130.2 0.0 reduce-scatter.13.cloned.1.call-start
  130.3 1.3 fusion.28
  131.5 0.7 copy-done.8
  132.2 5.2 convolution_convert_fusion.2
  137.5 0.0 reduce-scatter.13.cloned.1.call-update
  137.5 0.0 reduce-scatter.11.cloned.1.call-start
  137.5 2.7 fusion.27
  140.3 5.1 fusion.26
  145.4 7.7 add_convert_fusion
  153.2 0.0 reduce-scatter.11.cloned.1.call-update
  153.2 0.0 reduce-scatter.9.cloned.1.call-start
  153.2 0.9 copy-done.13
  154.1 5.2 convolution_convert_fusion
  159.3 0.0 reduce-scatter.9.cloned.1.call-update
  159.4 149.2 %reduce-scatter.15.cloned.1.call-done = bf16[288,128]{1,0:T(8,128)(2,1)} async-done(((bf16[4608,128]{1,0:T(8,128)(2,1)}), bf16[288,128]{1,0:T(8,128)(2,1)}) %reduce-scatter.15.cloned.1.call-update) | async-done | bytes 73744 | tf_op jit(solution)/shard_map/reduce_scatter | solution.py:88
  308.6 1.6 convert_element_type.148
  310.2 204.8 %reduce-scatter.17.cloned.1.call-done = bf16[288,128]{1,0:T(8,128)(2,1)} async-done(((bf16[4608,128]{1,0:T(8,128)(2,1)}), bf16[288,128]{1,0:T(8,128)(2,1)}) %reduce-scatter.17.cloned.1.call-update) | async-done | bytes 73744 | tf_op jit(solution)/shard_map/reduce_scatter | solution.py:91
  514.9 1.6 convert_element_type.150
  516.5 213.2 %reduce-scatter.19.cloned.1.call-done = bf16[288,256]{1,0:T(8,128)(2,1)} async-done(((bf16[4608,256]{1,0:T(8,128)(2,1)}), bf16[288,256]{1,0:T(8,128)(2,1)}) %reduce-scatter.19.cloned.1.call-update) | async-done | bytes 147472
  729.7 1.1 copy.36
  730.8 0.9 copy.26
  731.6 211.3 %reduce-scatter.13.cloned.1.call-done = bf16[288,256]{1,0:T(8,128)(2,1)} async-done(((bf16[4608,256]{1,0:T(8,128)(2,1)}), bf16[288,256]{1,0:T(8,128)(2,1)}) %reduce-scatter.13.cloned.1.call-update) | async-done | bytes 147472 | tf_op jit(solution)/shard_map/reduce_scatter | solution.py:85
  942.9 1.6 convert_element_type.146
  944.6 69.5 %reduce-scatter.11.cloned.1.call-done = bf16[32,4608]{1,0:T(8,128)(2,1)} async-done(((bf16[512,4608]{1,0:T(8,128)(2,1)}), bf16[32,4608]{1,0:T(8,128)(2,1)}) %reduce-scatter.11.cloned.1.call-update) | async-done | bytes 294928 | tf_op jit(solution)/shard_map/reduce_scatter | solution.py:71
  1014.1 1.2 fusion.23
  1015.3 70.3 %reduce-scatter.9.cloned.1.call-done = bf16[32,4608]{1,0:T(8,128)(2,1)} async-done(((bf16[512,4608]{1,0:T(8,128)(2,1)}), bf16[32,4608]{1,0:T(8,128)(2,1)}) %reduce-scatter.9.cloned.1.call-update) | async-done | bytes 294928 | tf_op jit(solution)/shard_map/reduce_scatter | solution.py:59
  1085.6 2.2 fusion.22
  (38 shorter events, 0.2 us)
Async XLA Ops:
  7.2 52.7 %copy-start = (bf16[4608,256]{1,0:T(8,128)(2,1)S(1)}, bf16[4608,256]{1,0:T(8,128)(2,1)}, u32[]{:S(2)}) copy-start(bf16[4608,256]{1,0:T(8,128)(2,1)} %param.9) | copy-start | bytes 7077892
  7.2 48.5 %all-gather.3.cloned.1.call-start = ((), (), s32[]{:S(2)}) async-start(), calls=%async_computation.6 | async-start | bytes 5013504 | tf_op jit(solution)/shard_map/all_gather | solution.py:54
  10.4 88.2 %all-gather.5.cloned.1.call-start = ((), (), s32[]{:S(2)}) async-start(), calls=%async_computation.8 | async-start | bytes 5013504 | tf_op jit(solution)/shard_map/all_gather | solution.py:66
  11.1 297.5 %reduce-scatter.15.cloned.1.call-start = ((), (), s32[]{:S(2)}) async-start(), calls=%async_computation.11 | async-start | bytes 1253376 | tf_op jit(solution)/shard_map/reduce_scatter | solution.py:88
  11.3 91.9 %copy-start.7 = (pred[512,512]{0,1:T(8,128)(4,1)}, pred[512,512]{0,1:T(8,128)(4,1)S(1)}, u32[]{:S(2)}) copy-start(pred[512,512]{0,1:T(8,128)(4,1)S(1)} %iota_compare_fusion) | copy-start | bytes 786436
  55.7 4.2 copy-start.1
  59.9 1.5 copy-start.16
  61.4 2.2 copy-start.14
  61.4 2.2 copy-start.4
  64.9 38.2 %copy-start.18 = (bf16[512,128,1]{1,0,2:T(8,128)(2,1)}, bf16[512,128,1]{1,0,2:T(8,128)(2,1)S(1)}, u32[]{:S(2)}) copy-start(bf16[512,128,1]{1,0,2:T(8,128)(2,1)S(1)} %fusion.12) | copy-start | bytes 393220
  98.5 4.7 copy-start.3
  98.5 8.5 slice-start
  103.2 1.0 copy-start.17
  103.2 3.8 slice-start.1
  104.2 2.4 copy-start.15
  109.5 405.4 %reduce-scatter.17.cloned.1.call-start = ((), (), s32[]{:S(2)}) async-start(), calls=%async_computation.12 | async-start | bytes 1253376 | tf_op jit(solution)/shard_map/reduce_scatter | solution.py:91
  112.0 0.7 copy-start.10
  117.5 612.2 %reduce-scatter.19.cloned.1.call-start = ((), (), s32[]{:S(2)}) async-start(), calls=%async_computation.13 | async-start | bytes 2506752
  120.1 0.7 copy-start.12
  130.2 812.7 %reduce-scatter.13.cloned.1.call-start = ((), (), s32[]{:S(2)}) async-start(), calls=%async_computation.10 | async-start | bytes 2506752 | tf_op jit(solution)/shard_map/reduce_scatter | solution.py:85
  131.5 0.7 copy-start.8
  137.5 2.8 copy-start.9
  137.5 876.6 %reduce-scatter.11.cloned.1.call-start = ((), (), s32[]{:S(2)}) async-start(), calls=%async_computation.9 | async-start | bytes 5013504 | tf_op jit(solution)/shard_map/reduce_scatter | solution.py:71
  140.3 5.2 copy-start.5
  140.3 5.1 copy-start.11
  153.2 1.0 copy-start.13
  153.2 932.4 %reduce-scatter.9.cloned.1.call-start = ((), (), s32[]{:S(2)}) async-start(), calls=%async_computation.7 | async-start | bytes 5013504 | tf_op jit(solution)/shard_map/reduce_scatter | solution.py:59
  159.4 854.7 %copy-start.2 = (bf16[32,4608]{1,0:T(8,128)(2,1)S(1)}, bf16[32,4608]{1,0:T(8,128)(2,1)}, u32[]{:S(2)}) copy-start(bf16[32,4608]{1,0:T(8,128)(2,1)} %param.7) | copy-start | bytes 884740
  159.4 926.2 %copy-start.6 = (bf16[32,4608]{1,0:T(8,128)(2,1)S(1)}, bf16[32,4608]{1,0:T(8,128)(2,1)}, u32[]{:S(2)}) copy-start(bf16[32,4608]{1,0:T(8,128)(2,1)} %param.13) | copy-start | bytes 884740
Sparse Core Ops, SparseCore 0:
  10.5 45.1 all-gather.2
  57.5 40.9 all-gather.4
  109.7 198.9 reduce-scatter.14
  312.8 202.0 reduce-scatter.16
  518.7 210.8 reduce-scatter.18
  733.5 209.3 reduce-scatter.12
  945.5 68.5 reduce-scatter.10
  1016.7 68.8 reduce-scatter.8
where the time goes:
time: 1100 us; the launch traced here: 1090 us
  waiting for transfers between devices  997 us (91%)
  matrix products  59.6 us (5%)
  between operations  14.5 us (1%)
  other arithmetic  13.7 us (1%)
    unnamed x9, waiting for transfers between devices  214 us
    reduce_scatter x1, waiting for transfers between devices, on_device(): lax.psum_scatter(inner_rows(normed, d_query).astype(jnp.bfloat16), 'dp',...  211 us
    reduce_scatter x1, waiting for transfers between devices, on_device(): lax.psum_scatter(inner_rows(normed, d_value).astype(jnp.bfloat16), 'dp',...  205 us
    reduce_scatter x1, waiting for transfers between devices, on_device(): lax.psum_scatter(inner_rows(normed, d_key).astype(jnp.bfloat16), 'dp', sc...  149 us
    reduce_scatter x1, waiting for transfers between devices, on_device(): lax.psum_scatter(jnp.dot(context, w_output, preferred_element_type=jnp.fl...  70.3 us
    reduce_scatter x1, waiting for transfers between devices, on_device(): lax.psum_scatter((term + right_trans(d_value, w_value)).astype(jnp.bfloat...  69.5 us
    all_gather x1, waiting for transfers between devices, on_device(): lax.all_gather(norm_rows(tokens, norm_gain), 'tensor', axis=0, tiled=True)  44.4 us
    all_gather x1, waiting for transfers between devices, on_device(): cotangent = lax.all_gather(d_mixed, 'tensor', axis=0, tiled=True)  33.6 us
  transfers between devices with their start and end apart: 8, of which 8 were waited for; matrix products, arithmetic and copies ran while one was open for 6% of the time, Pallas kernels for 0%

commit v1 on v0

v1 whole, which is shorter than its diff:
```python
import functools
import math

import jax
import jax.numpy as jnp
from jax import lax
from jax.experimental import pallas as pl
from jax.experimental.pallas import tpu as pltpu
from jax.sharding import PartitionSpec as P

D = 4608
HEADS = 32
HEAD = 128
SEQ = 512
ROWS = 32
QC = 256
CAP = 50.0
SCALE = 1.0 / math.sqrt(D // HEADS)
CHUNK = D // 8
HALF = D // 16
TILE = 512
MESH = pl.DeviceIdType.MESH
BF = jnp.bfloat16
F32 = jnp.float32

AB = (((1,), (0,)), ((), ()))
ABT = (((1,), (1,)), ((), ()))
ATB = (((0,), (0,)), ((), ()))


def dot(a, b, dims=AB):
    return lax.dot_general(a, b, dims, preferred_element_type=F32)


def at(i, n):
    return pl.ds(pl.multiple_of(i * n, n), n)


def kernel(
    tok, gain, wq, wk, wv, wo, dm,
    mixed_o, dtok_o, dwq_o, dwk_o, dwv_o, dwo_o,
    fn, fd, w, wout, qkv, ctx, dctx, dqkv, acc, probs, slope,
    grad, recv1, recv, recv_y, part, sib_in, far_in,
    w_sem, ag_s, ag_r, z_s, z_r, y_s, y_r, sib_s, sib_r, far_s, far_r,
):
    dp, tensor = lax.axis_index("dp"), lax.axis_index("tensor")
    z, yh = lax.div(dp, 2), lax.rem(dp, 2)
    yl, x, c = lax.div(tensor, 8), lax.rem(lax.div(tensor, 2), 4), lax.rem(tensor, 2)
    chip = yl * 4 + x

    def device(z_, yh_, yl_, x_, c_):
        return (z_ * 2 + yh_, yl_ * 8 + x_ * 2 + c_)

    def ring(i, step, n):
        return lax.rem(i + step + n, n)

    right = device(z, yh, yl, ring(x, 1, 4), c)
    left = device(z, yh, yl, ring(x, -1, 4), c)
    across = device(z, yh, 1 - yl, x, c)
    sibling = device(z, yh, yl, x, 1 - c)
    up = device(ring(z, 1, 8), yh, yl, x, c)
    down = device(ring(z, -1, 8), yh, yl, x, c)
    other_y = device(z, 1 - yh, yl, x, c)

    def chip_at(j):
        k = lax.rem(chip + j, 8)
        return k, device(z, yh, lax.div(k, 4), lax.rem(k, 4), c)

    weight_in = [
        pltpu.make_async_copy(wq, w.at[:, pl.ds(0, 256)], w_sem.at[0]),
        pltpu.make_async_copy(wk, w.at[:, pl.ds(256, 128)], w_sem.at[1]),
        pltpu.make_async_copy(wv, w.at[:, pl.ds(384, 128)], w_sem.at[2]),
        pltpu.make_async_copy(wo, wout, w_sem.at[3]),
    ]
    for copy in weight_in:
        copy.start()

    barrier = pltpu.get_barrier_semaphore()
    peers = [sibling, up, down, other_y] + [chip_at(j)[1] for j in range(1, 8)]
    for peer in peers:
        pl.semaphore_signal(barrier, inc=1, device_id=peer, device_id_type=MESH)

    values = tok[...].astype(F32)
    scale = lax.rsqrt(jnp.mean(values * values, axis=-1, keepdims=True) + 1e-06)
    mine = at(tensor, ROWS)
    fn[mine, :] = (values * scale * gain[...]).astype(BF)
    fd[mine, :] = dm[...]
    pl.semaphore_wait(barrier, len(peers))

    def block(dx, dy, core):
        return (yl if dy == 0 else 1 - yl) * 8 + ring(x, dx, 4) * 2 + core

    def gather(full, a):
        def copy(i, rows, to):
            return pltpu.make_async_remote_copy(
                src_ref=full.at[rows, :], dst_ref=full.at[rows, :],
                send_sem=ag_s.at[a, i], recv_sem=ag_r.at[a, i],
                device_id=to, device_id_type=MESH,
            )

        def whole(dx, dy, core=c):
            return at(block(dx, dy, core), ROWS)

        def first(dx):
            return at(block(dx, 0, c) * 2, ROWS // 2)

        def second(dx):
            return at(block(dx, 0, c) * 2 + 1, ROWS // 2)

        order = [(0, 0), (-1, 0), (1, 0), (0, 1), (2, 0), (-1, 1), (1, 1), (2, 1)]

        def to_sibling(i):
            copy(8 + i, whole(*order[i]), sibling).start()

        def step1():
            copy(2, whole(0, 0), across).start()
            copy(0, whole(0, 0), right).start()
            copy(1, whole(0, 0), left).start()
            to_sibling(0)

        def step2():
            copy(0, whole(-1, 0), right).wait_recv()
            copy(3, first(-1), right).start()
            copy(1, whole(1, 0), left).wait_recv()
            copy(4, second(1), left).start()
            copy(2, whole(0, 1), across).wait_recv()
            copy(5, whole(0, 1), right).start()
            copy(6, whole(0, 1), left).start()
            for i in (1, 2, 3):
                to_sibling(i)

        def step3():
            copy(3, first(2), right).wait_recv()
            copy(4, second(2), left).wait_recv()
            copy(7, whole(2, 0), across).start()
            to_sibling(4)

        def step4():
            copy(5, whole(-1, 1), right).wait_recv()
            to_sibling(5)
            copy(6, whole(1, 1), left).wait_recv()
            to_sibling(6)
            copy(7, whole(2, 1), across).wait_recv()
            to_sibling(7)

        def finish():
            for i in range(8):
                copy(8 + i, whole(*order[i], 1 - c), sibling).wait_recv()

        def sent():
            for i, to in ((0, right), (1, left), (2, across), (5, right), (6, left), (7, across)):
                copy(i, whole(0, 0), to).wait_send()
            copy(3, first(0), right).wait_send()
            copy(4, second(0), left).wait_send()
            for i in range(8):
                copy(8 + i, whole(0, 0), sibling).wait_send()

        return step1, step2, step3, step4, finish, sent

    n1, n2, n3, n4, n_end, n_sent = gather(fn, 0)
    d1, d2, d3, d4, d_end, d_sent = gather(fd, 1)
    n1()
    n2()
    d1()
    n3()
    n4()
    n_end()

    for copy in weight_in[:3]:
        copy.wait()
    acc[...] = jnp.zeros_like(acc)

    def project(i, carry):
        acc[...] += dot(fn[:, at(i, TILE)], w[at(i, TILE), :])
        return carry

    lax.fori_loop(0, D // TILE, project, 0)
    qkv[...] = acc[...].astype(BF)

    d2()

    blocks = ((0, 256), (256, 512))
    for h in range(2):
        for lo, hi in blocks:
            q = qkv[lo:hi, h * HEAD : (h + 1) * HEAD]
            scores = dot(q, qkv[:hi, 256:384], ABT)
            th = jnp.tanh(scores * (SCALE / CAP))
            row = lax.broadcasted_iota(jnp.int32, (256, hi), 0) + lo
            col = lax.broadcasted_iota(jnp.int32, (256, hi), 1)
            weight = jnp.where(row >= col, jnp.exp(CAP * th), 0.0)
            p = weight * (1.0 / jnp.sum(weight, axis=-1, keepdims=True))
            probs[h, lo:hi, :hi] = p
            slope[h, lo:hi, :hi] = p * ((1.0 - th * th) * SCALE)
            ctx[lo:hi, h * HEAD : (h + 1) * HEAD] = dot(
                p.astype(BF), qkv[:hi, 384:512]
            ).astype(BF)

    d3()

    def scatter(a):
        def sib_copy():
            return pltpu.make_async_remote_copy(
                src_ref=part.at[a, :, 1 - c], dst_ref=sib_in.at[a],
                send_sem=sib_s.at[a], recv_sem=sib_r.at[a],
                device_id=sibling, device_id_type=MESH,
            )

        def far_copy(j):
            k, to = chip_at(j)
            return pltpu.make_async_remote_copy(
                src_ref=part.at[a, k, c], dst_ref=far_in.at[a, j - 1],
                send_sem=far_s.at[a, j - 1], recv_sem=far_r.at[a, j - 1],
                device_id=to, device_id_type=MESH,
            )

        def start():
            sib_copy().start()

        def spread():
            sib_copy().wait()

            def one(k, carry):
                part[a, k, c] = (
                    part[a, k, c].astype(F32) + sib_in[a, k].astype(F32)
                ).astype(BF)
                return carry

            lax.fori_loop(0, 8, one, 0)
            for j in range(1, 8):
                far_copy(j).start()

        def total():
            for j in range(1, 8):
                far_copy(j).wait_recv()
            out = part[a, chip, c].astype(F32)
            for j in range(7):
                out = out + far_in[a, j].astype(F32)
            return out

        def sent():
            for j in range(1, 8):
                far_copy(j).wait_send()

        return start, spread, total, sent

    m_start, m_spread, m_total, m_sent = scatter(0)
    g_start, g_spread, g_total, g_sent = scatter(1)

    weight_in[3].wait()

    def mix(i, carry):
        term = dot(ctx[...], wout[:, at(i, TILE)])
        part[0, :, :, :, at(i, TILE)] = term.astype(BF).reshape(8, 2, ROWS, TILE)
        return carry

    lax.fori_loop(0, D // TILE, mix, 0)
    m_start()
    d4()
    d_end()

    acc[:, :QC] = jnp.zeros((SEQ, QC), F32)

    def back_out(i, carry):
        acc[:, :QC] += dot(fd[:, at(i, TILE)], wout[:, at(i, TILE)], ABT)
        return carry

    lax.fori_loop(0, D // TILE, back_out, 0)
    dctx[...] = acc[:, :QC].astype(BF)

    def z_chunk(k):
        return at(ring(z, k, 8), CHUNK)

    def z_half(k, b):
        return at(ring(z, k, 8) * 2 + b, HALF)

    def z_steps(p):
        def first_copy(way):
            return pltpu.make_async_remote_copy(
                src_ref=grad.at[p, z_half(4, way), :], dst_ref=recv1.at[p, way],
                send_sem=z_s.at[p, 0, way], recv_sem=z_r.at[p, 0, way],
                device_id=(up, down)[way], device_id_type=MESH,
            )

        def later_copy(s, way):
            return pltpu.make_async_remote_copy(
                src_ref=grad.at[p, z_chunk((4 - s) * (1 - 2 * way)), :],
                dst_ref=recv.at[p, s - 1, way],
                send_sem=z_s.at[p, s, way], recv_sem=z_r.at[p, s, way],
                device_id=(up, down)[way], device_id_type=MESH,
            )

        def y_copy():
            return pltpu.make_async_remote_copy(
                src_ref=grad.at[p, z_half(0, 1 - yh), :], dst_ref=recv_y.at[p],
                send_sem=y_s.at[p], recv_sem=y_r.at[p],
                device_id=other_y, device_id_type=MESH,
            )

        def start():
            for way in range(2):
                first_copy(way).start()

        def step(s):
            for way in range(2):
                if s == 1:
                    first_copy(way).wait_recv()
                    rows, arrived = z_half(3 * (1 - 2 * way), way), recv1[p, way]
                else:
                    later_copy(s - 1, way).wait_recv()
                    rows, arrived = z_chunk((4 - s) * (1 - 2 * way)), recv[p, s - 2, way]
                grad[p, rows, :] = (
                    grad[p, rows, :].astype(F32) + arrived.astype(F32)
                ).astype(BF)
                later_copy(s, way).start()

        def end():
            later_copy(3, 0).wait_recv()
            later_copy(3, 1).wait_recv()
            rows = z_chunk(0)
            grad[p, rows, :] = (
                grad[p, rows, :].astype(F32)
                + recv[p, 2, 0].astype(F32)
                + recv[p, 2, 1].astype(F32)
            ).astype(BF)
            y_copy().start()

        def total():
            y_copy().wait()
            return grad[p, z_half(0, yh), :].astype(F32) + recv_y[p].astype(F32)

        def sent():
            for way in range(2):
                first_copy(way).wait_send()
                for s in range(1, 4):
                    later_copy(s, way).wait_send()

        return start, step, end, total, sent

    o_start, o_step, o_end, o_total, o_sent = z_steps(0)
    q_start, q_step, q_end, q_total, q_sent = z_steps(1)
    k_start, k_step, k_end, k_total, k_sent = z_steps(2)

    def grad_out(i, carry):
        term = dot(fd[:, at(i, 256)], ctx[...], ATB)
        grad[0, at(i, 256), :] = term.astype(BF)
        return carry

    lax.fori_loop(0, D // 256, grad_out, 0)
    o_start()
    m_spread()

    acc[...] = jnp.zeros_like(acc)
    for h in range(2):
        for lo, hi in blocks:
            heads = slice(h * HEAD, (h + 1) * HEAD)
            d_ctx = dctx[lo:hi, heads]
            p = probs[h, lo:hi, :hi]
            d_p = dot(d_ctx, qkv[:hi, 384:512], ABT)
            inner = jnp.sum(p * d_p, axis=-1, keepdims=True)
            d_s = (slope[h, lo:hi, :hi] * (d_p - inner)).astype(BF)
            dqkv[lo:hi, heads] = dot(d_s, qkv[:hi, 256:384]).astype(BF)
            acc[:hi, 256:384] += dot(d_s, qkv[lo:hi, heads], ATB)
            acc[:hi, 384:512] += dot(p.astype(BF), d_ctx, ATB)
    dqkv[:, 256:512] = acc[:, 256:512].astype(BF)

    o_step(1)

    def grad_in(i, carry):
        term = dot(fn[:, at(i, 256)], dqkv[...], ATB).astype(BF)
        grad[1, at(i, 256), :] = term[:, :256]
        grad[2, at(i, 256), :] = term[:, 256:]
        return carry

    lax.fori_loop(0, D // 256, grad_in, 0)
    q_start()
    k_start()
    o_step(2)

    def back_in(i, carry):
        term = dot(dqkv[...], w[at(i, TILE), :], ABT)
        part[1, :, :, :, at(i, TILE)] = term.astype(BF).reshape(8, 2, ROWS, TILE)
        return carry

    lax.fori_loop(0, D // TILE, back_in, 0)
    g_start()
    q_step(1)
    k_step(1)
    o_step(3)
    g_spread()
    q_step(2)
    k_step(2)
    mixed_o[...] = (tok[...].astype(F32) + m_total()).astype(BF)
    o_end()
    q_step(3)
    k_step(3)

    d_normed = g_total()
    upstream = gain[...] * d_normed
    values = tok[...].astype(F32)
    scale = lax.rsqrt(jnp.mean(values * values, axis=-1, keepdims=True) + 1e-06)
    back_norm = scale * upstream - values * (scale * scale * scale) * jnp.mean(
        upstream * values, axis=-1, keepdims=True
    )
    dtok_o[...] = (dm[...].astype(F32) + back_norm).astype(BF)
    dwo_o[...] = o_total()

    q_end()
    k_end()
    dwq_o[...] = q_total()
    d_kv = k_total()
    dwk_o[...] = d_kv[:, :HEAD]
    dwv_o[...] = d_kv[:, HEAD:]

    for done in (n_sent, d_sent, m_sent, g_sent, o_sent, q_sent, k_sent):
        done()


def on_device(tokens, norm_gain, w_query, w_key, w_value, w_output, d_mixed):
    vmem = pl.BlockSpec(memory_space=pltpu.VMEM)
    hbm = pl.BlockSpec(memory_space=pl.ANY)
    dma = pltpu.SemaphoreType.DMA
    mixed, d_tokens, dw_query, dw_key, dw_value, dw_out_t = pl.pallas_call(
        kernel,
        out_shape=(
            jax.ShapeDtypeStruct((ROWS, D), BF),
            jax.ShapeDtypeStruct((ROWS, D), BF),
            jax.ShapeDtypeStruct((HALF, QC), F32),
            jax.ShapeDtypeStruct((HALF, HEAD), F32),
            jax.ShapeDtypeStruct((HALF, HEAD), F32),
            jax.ShapeDtypeStruct((HALF, QC), F32),
        ),
        in_specs=[vmem, vmem, hbm, hbm, hbm, hbm, vmem],
        out_specs=(vmem,) * 6,
        scratch_shapes=[
            pltpu.VMEM((SEQ, D), BF),
            pltpu.VMEM((SEQ, D), BF),
            pltpu.VMEM((D, 512), BF),
            pltpu.VMEM((QC, D), BF),
            pltpu.VMEM((SEQ, 512), BF),
            pltpu.VMEM((SEQ, QC), BF),
            pltpu.VMEM((SEQ, QC), BF),
            pltpu.VMEM((SEQ, 512), BF),
            pltpu.VMEM((SEQ, 512), F32),
            pltpu.VMEM((2, SEQ, SEQ), F32),
            pltpu.VMEM((2, SEQ, SEQ), F32),
            pltpu.VMEM((3, D, QC), BF),
            pltpu.VMEM((3, 2, HALF, QC), BF),
            pltpu.VMEM((3, 3, 2, CHUNK, QC), BF),
            pltpu.VMEM((3, HALF, QC), BF),
            pltpu.VMEM((2, 8, 2, ROWS, D), BF),
            pltpu.VMEM((2, 8, ROWS, D), BF),
            pltpu.VMEM((2, 7, ROWS, D), BF),
            dma((4,)),
            dma((2, 16)),
            dma((2, 16)),
            dma((3, 4, 2)),
            dma((3, 4, 2)),
            dma((3,)),
            dma((3,)),
            dma((2,)),
            dma((2,)),
            dma((2, 7)),
            dma((2, 7)),
        ],
        compiler_params=pltpu.CompilerParams(
            collective_id=0, has_side_effects=True, vmem_limit_bytes=64 * 2**20 - 2**17
        ),
        cost_estimate=pl.CostEstimate(
            flops=12 * 10**9, bytes_accessed=10**7, transcendentals=10**6
        ),
    )(tokens, norm_gain.reshape(1, D), w_query, w_key, w_value, w_output, d_mixed)
    return (mixed, d_tokens, dw_query, dw_key, dw_value, dw_out_t.T)


def solution(mesh):
    return jax.shard_map(
        on_device,
        mesh=mesh,
        in_specs=(
            P(("dp", "tensor"), None),
            P(),
            P(None, "tensor"),
            P(None, "tensor"),
            P(None, "tensor"),
            P("tensor", None),
            P(("dp", "tensor"), None),
        ),
        out_specs=(
            P(("dp", "tensor"), None),
            P(("dp", "tensor"), None),
            P("dp", "tensor"),
            P("dp", "tensor"),
            P("dp", "tensor"),
            P("tensor", "dp"),
        ),
        check_vma=False,
    )
```

time: 1100 us -> 150 us (0.14)
  waiting for transfers between devices: 997 us -> 0 us
  Pallas kernels: 0 us -> 139 us
  matrix products: 59.6 us -> 0 us
  between operations: 14.5 us -> 0.65 us
  other arithmetic: 13.7 us -> 0 us
    reduce_scatter x5 -> x0, waiting for transfers between devices: 705 us -> none  [the longest x1 211 us: on_device(): lax.psum_scatter(inner_rows(normed, d_query).astype(jnp.bfloat16), 'dp',...]
    unnamed x9 -> x0, waiting for transfers between devices: 214 us -> none
    pallas_call x0 -> x1, Pallas kernels: none -> 139 us  [on_device(): pl.pallas_call(kernel, out_shape=(jax.ShapeDtypeStruct((ROWS, D), BF), ja...]
    all_gather x2 -> x0, waiting for transfers between devices: 78 us -> none  [the longest x1 44.4 us: on_device(): lax.all_gather(norm_rows(tokens, norm_gain), 'tensor', axis=0, tiled=True)]
    dot_general x18 -> x0, matrix products: 59.6 us -> none  [the longest x4 20.2 us: right_trans(): lax.dot_general(left, right, (((1,), (1,)), ((), ())), preferred_element_...]
  transfers between devices with their start and end apart: 8 -> 0, of which waited for: 8 -> 0; matrix products, arithmetic and copies ran while one was open for 6% -> 0% of each run, Pallas kernels for 0% -> 0%
where the time goes in v1:
time: 150 us
  Pallas kernels  139 us (93%)
  local copies, waits for them, and re-layouts  10.3 us (7%)
    pallas_call x1, Pallas kernels, on_device(): pl.pallas_call(kernel, out_shape=(jax.ShapeDtypeStruct((ROWS, D), BF), ja...  139 us
    unnamed x8, local copies, waits for them, and re-layouts  9 us

profile of v1, /device:TPU:1, one launch (start us, length us, event | category | flops | bytes accessed | tf_op | source)
XLA Modules:
  0.0 149.8 jit_solution(15053468368061530534)
XLA Ops:
  0.6 1.3 reshape.15.gain
  2.0 138.8 %shard_map.118 = (bf16[32,4608]{1,0:T(8,128)(2,1)}, bf16[32,4608]{1,0:T(8,128)(2,1)}, f32[288,256]{1,0:T(8,128)}, f32[288,128]{1,0:T(8,128)}, f32[288,128]{1,0:T(8,128)}, /*index=5*/f32[288,256]{1,0:T(8,128)}) custom-call(bf16[32,4608]{1,0:T(8,128)(2,1)} %tok.1, f32[1,4608]{1,0:T(1,128)} %reshape.15.gain, bf16[4608,256]{1,0:T(8,128)(2,1)} %wq.1, ...), custom_call_target="tpu_custom_call" | custom-call | flops 12000000000 | bytes 10000000 | tf_op jit(solution)/shard_map/pallas_call | solution.py:422
  140.8 0.0 copy-start
  140.8 1.7 %copy.19 = bf16[32,4608]{1,0:T(8,128)(2,1)} copy(bf16[32,4608]{1,0:T(8,128)(2,1)} %get-tuple-element.24) | data formatting | bytes 589824
  142.6 1.7 %copy.20 = bf16[32,4608]{1,0:T(8,128)(2,1)} copy(bf16[32,4608]{1,0:T(8,128)(2,1)} %get-tuple-element.25) | data formatting | bytes 589824
  144.3 1.7 %copy.21 = f32[288,256]{1,0:T(8,128)} copy(f32[288,256]{1,0:T(8,128)} %get-tuple-element.26) | data formatting | bytes 589824
  146.0 1.6 %copy.22 = f32[288,128]{1,0:T(8,128)} copy(f32[288,128]{1,0:T(8,128)} %get-tuple-element.27) | data formatting | bytes 294912
  147.5 1.6 %copy.23 = f32[288,128]{1,0:T(8,128)} copy(f32[288,128]{1,0:T(8,128)} %get-tuple-element.28) | data formatting | bytes 294912
  149.1 0.0 copy-done
  149.1 0.7 copy.24
Async XLA Ops:
  140.8 8.3 %copy-start = (f32[288,256]{1,0:T(8,128)S(1)}, f32[288,256]{1,0:T(8,128)}, u32[]{:S(2)}) copy-start(f32[288,256]{1,0:T(8,128)} %get-tuple-element.17) | copy-start | bytes 884740

commit v2 on v1

v2 whole, which is shorter than its diff:
```python
import functools
import math

import jax
import jax.numpy as jnp
from jax import lax
from jax.experimental import pallas as pl
from jax.experimental.pallas import tpu as pltpu
from jax.sharding import PartitionSpec as P

D = 4608
HEADS = 32
HEAD = 128
SEQ = 512
ROWS = 32
QC = 256
CAP = 50.0
SCALE = 1.0 / math.sqrt(D // HEADS)
SIDE = D // 2
HALF = D // 16
TILE = 512
MESH = pl.DeviceIdType.MESH
BF = jnp.bfloat16
F32 = jnp.float32

AB = (((1,), (0,)), ((), ()))
ABT = (((1,), (1,)), ((), ()))
ATB = (((0,), (0,)), ((), ()))


def dot(a, b, dims=AB):
    return lax.dot_general(a, b, dims, preferred_element_type=F32)


def at(i, n):
    return pl.ds(pl.multiple_of(i * n, n), n)


def kernel(
    tok, gain, wq, wk, wv, wo, dm,
    mixed_o, dtok_o, dwq_o, dwk_o, dwv_o, dwo_o,
    fn, fd, fx, w, wout, qkv, ctx, dctx, dqkv, dqkv_x, acc, probs, slope,
    grad_o, grad_i, recv_o, recv_i, recv_y, part, sib_in, far_in,
    w_sem, ag_s, ag_r, zo_s, zo_r, zi_s, zi_r, y_s, y_r, sib_s, sib_r, far_s, far_r,
):
    dp, tensor = lax.axis_index("dp"), lax.axis_index("tensor")
    z, yh = lax.div(dp, 2), lax.rem(dp, 2)
    yl, x, c = lax.div(tensor, 8), lax.rem(lax.div(tensor, 2), 4), lax.rem(tensor, 2)

    def device(z_, yh_, yl_, x_, c_):
        return (z_ * 2 + yh_, yl_ * 8 + x_ * 2 + c_)

    def ring(i, step, n):
        return lax.rem(i + step + n, n)

    right = device(z, yh, yl, ring(x, 1, 4), c)
    left = device(z, yh, yl, ring(x, -1, 4), c)
    across = device(z, yh, 1 - yl, x, c)
    sibling = device(z, yh, yl, x, 1 - c)
    up = device(ring(z, 1, 8), yh, yl, x, c)
    down = device(ring(z, -1, 8), yh, yl, x, c)
    other_y = device(z, 1 - yh, yl, x, c)

    def remote(src, dst, send_sem, recv_sem, to):
        return pltpu.make_async_remote_copy(
            src_ref=src, dst_ref=dst, send_sem=send_sem, recv_sem=recv_sem,
            device_id=to, device_id_type=MESH,
        )

    columns = (pl.ds(0, 256), pl.ds(256, 128), pl.ds(384, 128))
    for i, weight in enumerate((wq, wk, wv)):
        for h in range(2):
            for k in range(8):
                pltpu.make_async_copy(
                    weight.at[pl.ds((2 * k + h) * HALF, HALF), :],
                    w.at[pl.ds((8 * h + k) * HALF, HALF), columns[i]],
                    w_sem.at[i],
                ).start()
    wout_in = pltpu.make_async_copy(wo, wout, w_sem.at[3])
    wout_in.start()

    barrier = pltpu.get_barrier_semaphore()
    peers = (sibling, left, right, across, up, down, other_y)
    for peer in peers:
        pl.semaphore_signal(barrier, inc=1, device_id=peer, device_id_type=MESH)

    values = tok[...].astype(F32)
    scale = lax.rsqrt(jnp.mean(values * values, axis=-1, keepdims=True) + 1e-06)
    normed = values * scale * gain[...]
    mine = at(tensor, ROWS)
    fn[mine, :] = jnp.concatenate(
        [
            normed[:, (2 * k + h) * HALF : (2 * k + h + 1) * HALF]
            for h in range(2)
            for k in range(8)
        ],
        axis=1,
    ).astype(BF)
    fd[mine, :] = dm[...]
    pl.semaphore_wait(barrier, len(peers))

    def block(dx, dy, core):
        return (yl if dy == 0 else 1 - yl) * 8 + ring(x, dx, 4) * 2 + core

    def gather(full, a):
        def copy(i, rows, to):
            return remote(
                full.at[rows, :], full.at[rows, :], ag_s.at[a, i], ag_r.at[a, i], to
            )

        def whole(dx, dy, core=c):
            return at(block(dx, dy, core), ROWS)

        def first(dx):
            return at(block(dx, 0, c) * 2, ROWS // 2)

        def second(dx):
            return at(block(dx, 0, c) * 2 + 1, ROWS // 2)

        order = [(0, 0), (-1, 0), (1, 0), (0, 1), (2, 0), (-1, 1), (1, 1), (2, 1)]

        def to_sibling(i):
            copy(8 + i, whole(*order[i]), sibling).start()

        def step1x():
            copy(0, whole(0, 0), right).start()
            copy(1, whole(0, 0), left).start()
            to_sibling(0)

        def step1y():
            copy(2, whole(0, 0), across).start()

        def step2():
            copy(0, whole(-1, 0), right).wait_recv()
            copy(3, first(-1), right).start()
            copy(1, whole(1, 0), left).wait_recv()
            copy(4, second(1), left).start()
            copy(2, whole(0, 1), across).wait_recv()
            copy(5, whole(0, 1), right).start()
            copy(6, whole(0, 1), left).start()
            for i in (1, 2, 3):
                to_sibling(i)

        def step3():
            copy(3, first(2), right).wait_recv()
            copy(4, second(2), left).wait_recv()
            copy(7, whole(2, 0), across).start()
            to_sibling(4)

        def step4():
            copy(5, whole(-1, 1), right).wait_recv()
            to_sibling(5)
            copy(6, whole(1, 1), left).wait_recv()
            to_sibling(6)
            copy(7, whole(2, 1), across).wait_recv()
            to_sibling(7)

        def finish():
            for i in range(8):
                copy(8 + i, whole(*order[i], 1 - c), sibling).wait_recv()

        def sent():
            for i, to in ((0, right), (1, left), (2, across), (5, right), (6, left), (7, across)):
                copy(i, whole(0, 0), to).wait_send()
            copy(3, first(0), right).wait_send()
            copy(4, second(0), left).wait_send()
            for i in range(8):
                copy(8 + i, whole(0, 0), sibling).wait_send()

        return step1x, step1y, step2, step3, step4, finish, sent

    n1x, n1y, n2, n3, n4, n_end, n_sent = gather(fn, 0)
    d1x, d1y, d2, d3, d4, d_end, d_sent = gather(fd, 1)
    x1x, x1y, x2, x3, x4, x_end, x_sent = gather(fx, 2)

    def side(h):
        return pl.ds(pl.multiple_of(h * SIDE, SIDE), SIDE)

    pair_rows = remote(
        fn.at[mine, side(1 - yh)], fx.at[mine, :], y_s.at[1], y_r.at[1], other_y
    )

    n1x()
    n1y()
    n2()
    d1x()
    pair_rows.start()
    n3()
    d1y()
    n4()
    n_end()

    for i, weight in enumerate((wq, wk, wv)):
        pltpu.make_async_copy(weight, w.at[:, columns[i]], w_sem.at[i]).wait()
    acc[...] = jnp.zeros_like(acc)

    def project(i, carry):
        acc[...] += dot(fn[:, at(i, TILE)], w[at(i, TILE), :])
        return carry

    lax.fori_loop(0, 5, project, 0)
    d2()
    lax.fori_loop(5, 9, project, 0)
    qkv[...] = acc[...].astype(BF)
    d3()
    pair_rows.wait_recv()
    x1x()
    x1y()

    blocks = ((0, 256), (256, 512))
    for h in range(2):
        for lo, hi in blocks:
            q = qkv[lo:hi, h * HEAD : (h + 1) * HEAD]
            scores = dot(q, qkv[:hi, 256:384], ABT)
            th = jnp.tanh(scores * (SCALE / CAP))
            row = lax.broadcasted_iota(jnp.int32, (256, hi), 0) + lo
            col = lax.broadcasted_iota(jnp.int32, (256, hi), 1)
            weight = jnp.where(row >= col, jnp.exp(CAP * th), 0.0)
            p = weight * (1.0 / jnp.sum(weight, axis=-1, keepdims=True))
            probs[h, lo:hi, :hi] = p
            slope[h, lo:hi, :hi] = p * ((1.0 - th * th) * SCALE)
            ctx[lo:hi, h * HEAD : (h + 1) * HEAD] = dot(
                p.astype(BF), qkv[:hi, 384:512]
            ).astype(BF)

    def scatter(a):
        def chip(dx, dy):
            return (yl if dy == 0 else 1 - yl) * 4 + ring(x, dx, 4)

        top, low = slice(0, ROWS // 2), slice(ROWS // 2, ROWS)

        def sib_copy():
            return remote(
                part.at[a, :, 1 - c], sib_in.at[a], sib_s.at[a], sib_r.at[a], sibling
            )

        def copy(i):
            dx, dy, slot, rows, to = (
                (2, 1, 0, None, across),
                (1, 1, 1, None, right),
                (-1, 1, 2, None, left),
                (2, 0, 3, top, right),
                (2, 0, 3, low, left),
                (1, 0, 4, None, right),
                (-1, 0, 5, None, left),
                (0, 1, 6, None, across),
            )[i]
            src, dst = part.at[a, chip(dx, dy), c], far_in.at[a, slot]
            if rows is not None:
                src, dst = src.at[rows], dst.at[rows]
            return remote(src, dst, far_s.at[a, i], far_r.at[a, i], to)

        def add(dx, dy, slots, rows=slice(0, ROWS)):
            k = chip(dx, dy)
            total = part[a, k, c, rows].astype(F32)
            for slot in slots:
                total = total + far_in[a, slot, rows].astype(F32)
            part[a, k, c, rows] = total.astype(BF)

        def start():
            sib_copy().start()

        def spread():
            sib_copy().wait()

            def one(k, carry):
                part[a, k, c] = (
                    part[a, k, c].astype(F32) + sib_in[a, k].astype(F32)
                ).astype(BF)
                return carry

            lax.fori_loop(0, 8, one, 0)
            for i in range(3):
                copy(i).start()

        def middle():
            copy(0).wait_recv()
            add(2, 0, (0,))
            copy(3).start()
            copy(4).start()
            copy(1).wait_recv()
            copy(2).wait_recv()
            add(0, 1, (1, 2))
            copy(7).start()

        def late():
            copy(3).wait_recv()
            add(1, 0, (3,), top)
            copy(5).start()
            copy(4).wait_recv()
            add(-1, 0, (3,), low)
            copy(6).start()

        def total():
            out = part[a, chip(0, 0), c].astype(F32)
            for i, slot in ((5, 4), (6, 5), (7, 6)):
                copy(i).wait_recv()
                out = out + far_in[a, slot].astype(F32)
            return out

        def sent():
            for i in range(8):
                copy(i).wait_send()

        return start, spread, middle, late, total, sent

    m_start, m_spread, m_middle, m_late, m_total, m_sent = scatter(0)
    g_start, g_spread, g_middle, g_late, g_total, g_sent = scatter(1)

    wout_in.wait()

    def mix(i, carry):
        term = dot(ctx[...], wout[:, at(i, TILE)])
        part[0, :, :, :, at(i, TILE)] = term.astype(BF).reshape(8, 2, ROWS, TILE)
        return carry

    lax.fori_loop(0, D // TILE, mix, 0)
    m_start()
    d4()
    x2()
    d_end()

    away = (4, 3, 3, 2, 2, 1, 1)

    def z_steps(grad, recv, send_sem, recv_sem, rows):
        half = rows // 2

        def place(i, way, distance):
            part_of = way if i % 2 == 0 else 1 - way
            return at(ring(z, distance * (1 - 2 * way), 8) * 2 + part_of, half)

        def copy(i, way):
            return remote(
                grad.at[place(i, way, away[i]), :], recv.at[i, way],
                send_sem.at[i, way], recv_sem.at[i, way], (up, down)[way],
            )

        def arrive(i, way):
            copy(i, way).wait_recv()
            here = place(i, way, away[i] - 1)
            grad[here, :] = (
                grad[here, :].astype(F32) + recv[i, way].astype(F32)
            ).astype(BF)

        def start():
            for i in range(2):
                for way in range(2):
                    copy(i, way).start()

        def step(i):
            for way in range(2):
                arrive(i - 2, way)
                copy(i, way).start()

        def end():
            for i in (5, 6):
                for way in range(2):
                    arrive(i, way)

        def sent():
            for i in range(7):
                for way in range(2):
                    copy(i, way).wait_send()

        return start, step, end, sent

    o_start, o_step, o_end, o_sent = z_steps(grad_o, recv_o, zo_s, zo_r, 2 * HALF)
    q_start, q_step, q_end, q_sent = z_steps(
        grad_i.at[0], recv_i.at[0], zi_s.at[0], zi_r.at[0], HALF
    )
    k_start, k_step, k_end, k_sent = z_steps(
        grad_i.at[1], recv_i.at[1], zi_s.at[1], zi_r.at[1], HALF
    )

    def grad_out(i, carry):
        term = dot(fd[:, at(i, 256)], ctx[...], ATB)
        grad_o[at(i, 256), :] = term.astype(BF)
        return carry

    lax.fori_loop(0, D // 256, grad_out, 0)
    o_start()

    acc[:, :QC] = jnp.zeros((SEQ, QC), F32)

    def back_out(i, carry):
        acc[:, :QC] += dot(fd[:, at(i, TILE)], wout[:, at(i, TILE)], ABT)
        return carry

    lax.fori_loop(0, D // TILE, back_out, 0)
    dctx[...] = acc[:, :QC].astype(BF)
    x3()
    m_spread()
    o_step(2)

    def pair_copy(i):
        cols = (pl.ds(0, 128), pl.ds(128, 128), pl.ds(256, 256))[i]
        return remote(
            dqkv.at[:, cols], dqkv_x.at[:, cols], y_s.at[2 + i], y_r.at[2 + i], other_y
        )

    acc[...] = jnp.zeros_like(acc)
    for h in range(2):
        for lo, hi in blocks:
            heads = slice(h * HEAD, (h + 1) * HEAD)
            d_ctx = dctx[lo:hi, heads]
            p = probs[h, lo:hi, :hi]
            d_p = dot(d_ctx, qkv[:hi, 384:512], ABT)
            inner = jnp.sum(p * d_p, axis=-1, keepdims=True)
            d_s = (slope[h, lo:hi, :hi] * (d_p - inner)).astype(BF)
            dqkv[lo:hi, heads] = dot(d_s, qkv[:hi, 256:384]).astype(BF)
            acc[:hi, 256:384] += dot(d_s, qkv[lo:hi, heads], ATB)
            acc[:hi, 384:512] += dot(p.astype(BF), d_ctx, ATB)
        pair_copy(h).start()
        if h == 0:
            x4()
            o_step(3)
    dqkv[:, 256:512] = acc[:, 256:512].astype(BF)
    pair_copy(2).start()
    o_step(4)
    m_middle()

    def back_in(i, carry):
        term = dot(dqkv[...], w[at(i, TILE), :], ABT)
        part[1, :, :, :, at(i, TILE)] = term.astype(BF).reshape(8, 2, ROWS, TILE)
        return carry

    lax.fori_loop(0, D // TILE, back_in, 0)
    g_start()
    o_step(5)
    m_late()
    g_spread()
    o_step(6)
    x_end()
    for i in range(3):
        pair_copy(i).wait_recv()

    def grad_in(i, carry):
        own = pl.ds(pl.multiple_of(yh * SIDE + i * 256, 256), 256)
        term = dot(fn[:, own], dqkv[...], ATB) + dot(fx[:, at(i, 256)], dqkv_x[...], ATB)
        term = term.astype(BF)
        grad_i[0, at(i, 256), :] = term[:, :256]
        grad_i[1, at(i, 256), :] = term[:, 256:]
        return carry

    lax.fori_loop(0, SIDE // 256, grad_in, 0)
    q_start()
    k_start()

    def keep(h):
        return at(z * 2 + h, HALF)

    o_end()
    y_copy = remote(grad_o.at[keep(1 - yh), :], recv_y, y_s.at[0], y_r.at[0], other_y)
    y_copy.start()
    q_step(2)
    k_step(2)
    g_middle()
    q_step(3)
    k_step(3)
    mixed_o[...] = (tok[...].astype(F32) + m_total()).astype(BF)
    q_step(4)
    k_step(4)
    g_late()
    q_step(5)
    k_step(5)
    y_copy.wait_recv()
    dwo_o[...] = grad_o[keep(yh), :].astype(F32) + recv_y[...].astype(F32)
    q_step(6)
    k_step(6)

    summed = g_total()
    d_normed = jnp.concatenate(
        [
            summed[:, (8 * h + k) * HALF : (8 * h + k + 1) * HALF]
            for k in range(8)
            for h in range(2)
        ],
        axis=1,
    )
    upstream = gain[...] * d_normed
    values = tok[...].astype(F32)
    scale = lax.rsqrt(jnp.mean(values * values, axis=-1, keepdims=True) + 1e-06)
    back_norm = scale * upstream - values * (scale * scale * scale) * jnp.mean(
        upstream * values, axis=-1, keepdims=True
    )
    dtok_o[...] = (dm[...].astype(F32) + back_norm).astype(BF)

    q_end()
    k_end()
    dwq_o[...] = grad_i[0, at(z, HALF), :].astype(F32)
    dwk_o[...] = grad_i[1, at(z, HALF), :HEAD].astype(F32)
    dwv_o[...] = grad_i[1, at(z, HALF), HEAD:].astype(F32)

    for done in (n_sent, d_sent, x_sent, m_sent, g_sent, o_sent, q_sent, k_sent):
        done()
    pair_rows.wait_send()
    y_copy.wait_send()
    for i in range(3):
        pair_copy(i).wait_send()


def hand_out(*refs):
    sources, results, held, sem = refs[:6], refs[6:12], refs[12:18], refs[18]
    loads = [
        pltpu.make_async_copy(source, ref, sem.at[0, i])
        for i, (source, ref) in enumerate(zip(sources, held))
    ]
    stores = [
        pltpu.make_async_copy(ref, result, sem.at[1, i])
        for i, (ref, result) in enumerate(zip(held, results))
    ]
    for load in loads:
        load.start()
    for load, store in zip(loads, stores):
        load.wait()
        store.start()
    for store in stores:
        store.wait()


def on_device(tokens, norm_gain, w_query, w_key, w_value, w_output, d_mixed):
    vmem = pl.BlockSpec(memory_space=pltpu.VMEM)
    hbm = pl.BlockSpec(memory_space=pl.ANY)
    dma = pltpu.SemaphoreType.DMA
    results = (
        jax.ShapeDtypeStruct((ROWS, D), BF),
        jax.ShapeDtypeStruct((ROWS, D), BF),
        jax.ShapeDtypeStruct((HALF, QC), F32),
        jax.ShapeDtypeStruct((HALF, HEAD), F32),
        jax.ShapeDtypeStruct((HALF, HEAD), F32),
        jax.ShapeDtypeStruct((HALF, QC), F32),
    )
    made = pl.pallas_call(
        kernel,
        out_shape=results,
        in_specs=[vmem, vmem, hbm, hbm, hbm, hbm, vmem],
        out_specs=(vmem,) * 6,
        scratch_shapes=[
            pltpu.VMEM((SEQ, D), BF),
            pltpu.VMEM((SEQ, D), BF),
            pltpu.VMEM((SEQ, SIDE), BF),
            pltpu.VMEM((D, 512), BF),
            pltpu.VMEM((QC, D), BF),
            pltpu.VMEM((SEQ, 512), BF),
            pltpu.VMEM((SEQ, QC), BF),
            pltpu.VMEM((SEQ, QC), BF),
            pltpu.VMEM((SEQ, 512), BF),
            pltpu.VMEM((SEQ, 512), BF),
            pltpu.VMEM((SEQ, 512), F32),
            pltpu.VMEM((2, SEQ, SEQ), F32),
            pltpu.VMEM((2, SEQ, SEQ), F32),
            pltpu.VMEM((D, QC), BF),
            pltpu.VMEM((2, SIDE, QC), BF),
            pltpu.VMEM((7, 2, HALF, QC), BF),
            pltpu.VMEM((2, 7, 2, HALF // 2, QC), BF),
            pltpu.VMEM((HALF, QC), BF),
            pltpu.VMEM((2, 8, 2, ROWS, D), BF),
            pltpu.VMEM((2, 8, ROWS, D), BF),
            pltpu.VMEM((2, 7, ROWS, D), BF),
            dma((4,)),
            dma((3, 16)),
            dma((3, 16)),
            dma((7, 2)),
            dma((7, 2)),
            dma((2, 7, 2)),
            dma((2, 7, 2)),
            dma((5,)),
            dma((5,)),
            dma((2,)),
            dma((2,)),
            dma((2, 8)),
            dma((2, 8)),
        ],
        compiler_params=pltpu.CompilerParams(
            collective_id=0, has_side_effects=True, vmem_limit_bytes=64 * 2**20 - 2**17
        ),
        cost_estimate=pl.CostEstimate(
            flops=12 * 10**9, bytes_accessed=10**7, transcendentals=10**6
        ),
    )(tokens, norm_gain, w_query, w_key, w_value, w_output, d_mixed)
    mixed, d_tokens, dw_query, dw_key, dw_value, dw_out_t = pl.pallas_call(
        hand_out,
        out_shape=results,
        in_specs=[pl.BlockSpec(memory_space=pltpu.HBM)] * 6,
        out_specs=(pl.BlockSpec(memory_space=pltpu.HBM),) * 6,
        scratch_shapes=[pltpu.VMEM(r.shape, r.dtype) for r in results] + [dma((2, 6))],
    )(*made)
    return (mixed, d_tokens, dw_query, dw_key, dw_value, dw_out_t.T)


def solution(mesh):
    return jax.shard_map(
        on_device,
        mesh=mesh,
        in_specs=(
            P(("dp", "tensor"), None),
            P(),
            P(None, "tensor"),
            P(None, "tensor"),
            P(None, "tensor"),
            P("tensor", None),
            P(("dp", "tensor"), None),
        ),
        out_specs=(
            P(("dp", "tensor"), None),
            P(("dp", "tensor"), None),
            P("dp", "tensor"),
            P("dp", "tensor"),
            P("dp", "tensor"),
            P("tensor", "dp"),
        ),
        check_vma=False,
    )
```

time: 150 us -> 119 us (0.79)
  Pallas kernels: 139 us -> 119 us
  local copies, waits for them, and re-layouts: 10.3 us -> 0 us
    pallas_call x1 -> x2, Pallas kernels: 139 us -> 119 us  [the longest x1 116 us: on_device(): pl.pallas_call(kernel, out_shape=results, in_specs=[vmem, vmem, hbm, hbm,...]
    unnamed x8 -> x0, local copies, waits for them, and re-layouts: 9 us -> none
where the time goes in v2:
time: 119 us
  Pallas kernels  119 us (100%)
    pallas_call x1, Pallas kernels, on_device(): pl.pallas_call(kernel, out_shape=results, in_specs=[vmem, vmem, hbm, hbm,...  116 us

profile of v2, /device:TPU:1, one launch (start us, length us, event | category | flops | bytes accessed | tf_op | source)
XLA Modules:
  0.0 119.3 jit_solution(6553306005035652300)
XLA Ops:
  0.6 116.5 %shard_map.118 = (bf16[32,4608]{1,0:T(8,128)(2,1)}, bf16[32,4608]{1,0:T(8,128)(2,1)}, f32[288,256]{1,0:T(8,128)}, f32[288,128]{1,0:T(8,128)}, f32[288,128]{1,0:T(8,128)}, /*index=5*/f32[288,256]{1,0:T(8,128)}) custom-call(bf16[32,4608]{1,0:T(8,128)(2,1)} %tok.1, f32[4608]{0:T(1024)} %gain.1, bf16[4608,256]{1,0:T(8,128)(2,1)} %wq.1, bf16[4608,128]{1,0:T(8,128)(2,1)} %wk.1, ...), custom_call_target="tpu_custom_call" | custom-call | flops 12000000000 | bytes 10000000 | tf_op jit(solution)/shard_map/pallas_call | solution.py:533
  117.1 2.2 %shard_map.119 = (bf16[32,4608]{1,0:T(8,128)(2,1)}, bf16[32,4608]{1,0:T(8,128)(2,1)}, f32[288,256]{1,0:T(8,128)}, f32[288,128]{1,0:T(8,128)}, f32[288,128]{1,0:T(8,128)}, /*index=5*/f32[288,256]{1,0:T(8,128)}) custom-call(bf16[32,4608]{1,0:T(8,128)(2,1)} %get-tuple-element.18.refs_0_, bf16[32,4608]{1,0:T(8,128)(2,1)} %get-tuple-element.19.refs_1_, ...), custom_call_target="tpu_custom_call" | custom-call | tf_op jit(solution)/shard_map/pallas_call | solution.py:581

commit v3 on v0

v3 whole, which is shorter than its diff:
```python
import functools
import math

import jax
import jax.numpy as jnp
from jax import lax
from jax.experimental import pallas as pl
from jax.experimental.pallas import tpu as pltpu
from jax.sharding import PartitionSpec as P

D = 4608
HEADS = 32
HEAD = 128
SEQ = 512
ROWS = 32
QC = 256
CAP = 50.0
SCALE = 1.0 / math.sqrt(D // HEADS)
SIDE = D // 2
HALF = D // 16
THIRD = D // 3
QUARTER = D // 4
MESH = pl.DeviceIdType.MESH
BF = jnp.bfloat16
F32 = jnp.float32

AB = (((1,), (0,)), ((), ()))
ABT = (((1,), (1,)), ((), ()))
ATB = (((0,), (0,)), ((), ()))


def dot(a, b, dims=AB):
    return lax.dot_general(a, b, dims, preferred_element_type=F32)


def at(i, n):
    return pl.ds(pl.multiple_of(i * n, n), n)


def kernel(
    tok_h, gain_h, wq, wk, wv, wo, dm_h,
    mixed_o, dtok_o, dwq_o, dwk_o, dwv_o, dwo_o,
    tok, gain, dm, mixed, dtok, dwq, dwk, dwv, dwo, mix_sum,
    fn, fd, fx, w, wout, qkv, ctx, ctx_t, dctx, dqkv, dqkv_x, acc, probs, slope,
    grad_o, grad_i, recv_o, recv_i, recv_y, part, sib_in, far_in,
    in_sem, out_sem, ag_s, ag_r, hi_s, hi_r, zo_s, zo_r, zi_s, zi_r, y_s, y_r, sib_s, sib_r, far_s, far_r,
):
    dp, tensor = lax.axis_index("dp"), lax.axis_index("tensor")
    z, yh = lax.div(dp, 2), lax.rem(dp, 2)
    yl, x, c = lax.div(tensor, 8), lax.rem(lax.div(tensor, 2), 4), lax.rem(tensor, 2)

    def device(z_, yh_, yl_, x_, c_):
        return (z_ * 2 + yh_, yl_ * 8 + x_ * 2 + c_)

    def ring(i, step, n):
        return lax.rem(i + step + n, n)

    right = device(z, yh, yl, ring(x, 1, 4), c)
    left = device(z, yh, yl, ring(x, -1, 4), c)
    across = device(z, yh, 1 - yl, x, c)
    sibling = device(z, yh, yl, x, 1 - c)
    up = device(ring(z, 1, 8), yh, yl, x, c)
    down = device(ring(z, -1, 8), yh, yl, x, c)
    other_y = device(z, 1 - yh, yl, x, c)
    next_y = device(z, 1 - yh, 1 - yl, x, c)

    lead = lax.div(ring(z, 3, 8), 2)

    def quarter(j):
        return at(lax.rem(lead + j, 4), QUARTER)

    barrier = pltpu.get_barrier_semaphore()
    peers = (sibling, left, right, across, up, down, other_y, next_y)
    for peer in peers:
        pl.semaphore_signal(barrier, inc=1, device_id=peer, device_id_type=MESH)
    tok_in = pltpu.make_async_copy(tok_h, tok, in_sem.at[0])
    gain_in = pltpu.make_async_copy(gain_h, gain, in_sem.at[1])
    dm_in = pltpu.make_async_copy(dm_h, dm, in_sem.at[2])
    for copy in (tok_in, gain_in, dm_in):
        copy.start()

    def remote(src, dst, send_sem, recv_sem, to):
        return pltpu.make_async_remote_copy(
            src_ref=src, dst_ref=dst, send_sem=send_sem, recv_sem=recv_sem,
            device_id=to, device_id_type=MESH,
        )

    tok_in.wait()
    gain_in.wait()
    values = tok[...].astype(F32)
    scale = lax.rsqrt(jnp.mean(values * values, axis=-1, keepdims=True) + 1e-06)
    normed = values * scale * gain[...]
    mine = at(tensor, ROWS)
    sides = [
        jnp.concatenate(
            [normed[:, (2 * k + h) * HALF : (2 * k + h + 1) * HALF] for k in range(8)], axis=1
        )
        for h in range(2)
    ]
    fn[mine, :SIDE] = jnp.where(yh == 0, sides[1], sides[0]).astype(BF)
    fn[mine, SIDE:] = jnp.where(yh == 0, sides[0], sides[1]).astype(BF)
    dm_in.wait()
    for j in range(4):
        fd[mine, j * QUARTER : (j + 1) * QUARTER] = dm[:, quarter(j)]
    pl.semaphore_wait(barrier, len(peers))

    def block(dx, dy, core):
        return (yl if dy == 0 else 1 - yl) * 8 + ring(x, dx, 4) * 2 + core

    class Gather:
        order = ((0, 0), (-1, 0), (1, 0), (0, 1), (2, 0), (-1, 1), (1, 1), (2, 1))

        def __init__(self, full, a, first_column, columns):
            self.full, self.a = full, a
            self.columns = pl.ds(first_column, columns)

        def copy(self, i, rows, to):
            ref = self.full.at[rows, self.columns]
            return remote(ref, ref, ag_s.at[self.a, i], ag_r.at[self.a, i], to)

        def whole(self, dx, dy, core=c):
            return at(block(dx, dy, core), ROWS)

        def piece(self, dx, half):
            return at(block(dx, 0, c) * 2 + half, ROWS // 2)

        def to_sibling(self, i):
            self.copy(8 + i, self.whole(*self.order[i]), sibling).start()

        def step1(self):
            self.copy(0, self.whole(0, 0), right).start()
            self.copy(1, self.whole(0, 0), left).start()
            self.copy(2, self.whole(0, 0), across).start()
            self.to_sibling(0)

        def step2(self):
            self.copy(0, self.whole(-1, 0), right).wait_recv()
            self.copy(3, self.piece(-1, 0), right).start()
            self.copy(1, self.whole(1, 0), left).wait_recv()
            self.copy(4, self.piece(1, 1), left).start()
            self.copy(2, self.whole(0, 1), across).wait_recv()
            self.copy(5, self.whole(0, 1), right).start()
            self.copy(6, self.whole(0, 1), left).start()
            for i in (1, 2, 3):
                self.to_sibling(i)

        def step3(self):
            self.copy(3, self.piece(2, 0), right).wait_recv()
            self.copy(4, self.piece(2, 1), left).wait_recv()
            self.copy(7, self.whole(2, 0), across).start()
            self.to_sibling(4)

        def step4(self):
            self.copy(5, self.whole(-1, 1), right).wait_recv()
            self.to_sibling(5)
            self.copy(6, self.whole(1, 1), left).wait_recv()
            self.to_sibling(6)
            self.copy(7, self.whole(2, 1), across).wait_recv()
            self.to_sibling(7)

        def end(self):
            for i in range(8):
                self.copy(8 + i, self.whole(*self.order[i], 1 - c), sibling).wait_recv()

        def sent(self):
            for i, to in ((0, right), (1, left), (2, across), (5, right), (6, left), (7, across)):
                self.copy(i, self.whole(0, 0), to).wait_send()
            self.copy(3, self.piece(0, 0), right).wait_send()
            self.copy(4, self.piece(0, 0), left).wait_send()
            for i in range(8):
                self.copy(8 + i, self.whole(0, 0), sibling).wait_send()

    n = [Gather(fn, t, t * THIRD, THIRD) for t in range(3)]
    d_parts = ((0, 2 * QUARTER), (2 * QUARTER, QUARTER), (3 * QUARTER, QUARTER))
    d = [Gather(fd, 3 + t, *d_parts[t]) for t in range(3)]

    pieces = ((0, THIRD), (THIRD, SIDE - THIRD))

    def from_next(i):
        ref = (at(c, SEQ // 2), pl.ds(*pieces[i]))
        return remote(fn.at[ref], fx.at[ref], hi_s.at[i], hi_r.at[i], next_y)

    def from_sibling(i):
        ref = fx.at[at(c, SEQ // 2), pl.ds(*pieces[i])]
        return remote(ref, ref, hi_s.at[2 + i], hi_r.at[2 + i], sibling)

    def third(t):
        return slice(t * THIRD, (t + 1) * THIRD)

    def project(t):
        term = dot(fn[:, third(t)], w[third(t), :])
        if t == 0:
            acc[...] = term
        elif t == 1:
            acc[...] += term
        else:
            qkv[...] = (acc[...] + term).astype(BF)

    n[0].step1()
    n[1].step1()

    columns = (pl.ds(0, 256), pl.ds(256, 128), pl.ds(384, 128))
    for i, weight in enumerate((wq, wk, wv)):
        for h in range(2):
            for k in range(8):
                pltpu.make_async_copy(
                    weight.at[at(2 * k + lax.rem(yh + 1 + h, 2), HALF), :],
                    w.at[pl.ds((8 * h + k) * HALF, HALF), columns[i]],
                    in_sem.at[3 + i],
                ).start()
    for j in range(4):
        pltpu.make_async_copy(
            wo.at[:, quarter(j)], wout.at[:, pl.ds(j * QUARTER, QUARTER)], in_sem.at[6]
        ).start()

    n[0].step2()
    n[2].step1()
    n[0].step3()
    n[1].step2()
    d[0].step1()
    n[0].step4()
    n[1].step3()
    n[2].step2()
    n[0].end()
    for i, weight in enumerate((wq, wk, wv)):
        pltpu.make_async_copy(weight, w.at[:, columns[i]], in_sem.at[3 + i]).wait()
    project(0)
    from_next(0).start()
    n[1].step4()
    d[1].step1()
    n[2].step3()
    n[1].end()
    from_next(1).start()
    project(1)
    d[0].step2()
    n[2].step4()
    d[2].step1()
    n[2].end()
    project(2)

    blocks = ((0, 256), (256, 512))

    def attend(h):
        for lo, hi in blocks:
            q = qkv[lo:hi, h * HEAD : (h + 1) * HEAD]
            scores = dot(q, qkv[:hi, 256:384], ABT)
            th = jnp.tanh(scores * (SCALE / CAP))
            row = lax.broadcasted_iota(jnp.int32, (256, hi), 0) + lo
            col = lax.broadcasted_iota(jnp.int32, (256, hi), 1)
            weight = jnp.where(row >= col, jnp.exp(CAP * th), 0.0)
            p = weight * (1.0 / jnp.sum(weight, axis=-1, keepdims=True))
            probs[h, lo:hi, :hi] = p
            slope[h, lo:hi, :hi] = p * ((1.0 - th * th) * SCALE)
            ctx[lo:hi, h * HEAD : (h + 1) * HEAD] = dot(
                p.astype(BF), qkv[:hi, 384:512]
            ).astype(BF)

    attend(0)
    d[0].step3()
    d[1].step2()
    attend(1)
    ctx_t[...] = ctx[...].T

    class Scatter:
        moves = (
            (2, 1, 0, None, across),
            (1, 1, 1, None, right),
            (-1, 1, 2, None, left),
            (2, 0, 3, 0, right),
            (2, 0, 3, 1, left),
            (1, 0, 4, None, right),
            (-1, 0, 5, None, left),
            (0, 1, 6, None, across),
        )

        def __init__(self, a, t):
            self.a, self.t = a, t
            self.part, self.far = part.at[a, t], far_in.at[a, t]

        def chip(self, dx, dy):
            return (yl if dy == 0 else 1 - yl) * 4 + ring(x, dx, 4)

        def sib_copy(self):
            a, t = self.a, self.t
            return remote(
                part.at[a, t, :, 1 - c], sib_in.at[a, t], sib_s.at[a, t], sib_r.at[a, t], sibling
            )

        def copy(self, i):
            dx, dy, slot, half, to = self.moves[i]
            src, dst = self.part.at[self.chip(dx, dy), c], self.far.at[slot]
            if half is not None:
                rows = pl.ds(half * (ROWS // 2), ROWS // 2)
                src, dst = src.at[rows], dst.at[rows]
            return remote(src, dst, far_s.at[self.a, self.t, i], far_r.at[self.a, self.t, i], to)

        def add(self, dx, dy, slots, rows=slice(0, ROWS)):
            a, t, k = self.a, self.t, self.chip(dx, dy)
            total = part[a, t, k, c, rows].astype(F32)
            for slot in slots:
                total = total + far_in[a, t, slot, rows].astype(F32)
            part[a, t, k, c, rows] = total.astype(BF)

        def start(self, term):
            part[self.a, self.t] = term.astype(BF).reshape(8, 2, ROWS, THIRD)
            self.sib_copy().start()

        def spread(self):
            a, t = self.a, self.t
            self.sib_copy().wait()

            def one(k, carry):
                part[a, t, k, c] = part[a, t, k, c] + sib_in[a, t, k]
                return carry

            lax.fori_loop(0, 8, one, 0)
            for i in range(3):
                self.copy(i).start()

        def middle(self):
            self.copy(0).wait_recv()
            self.add(2, 0, (0,))
            self.copy(3).start()
            self.copy(4).start()
            self.copy(1).wait_recv()
            self.copy(2).wait_recv()
            self.add(0, 1, (1, 2))
            self.copy(7).start()

        def late(self):
            self.copy(3).wait_recv()
            self.add(1, 0, (3,), slice(0, ROWS // 2))
            self.copy(5).start()
            self.copy(4).wait_recv()
            self.add(-1, 0, (3,), slice(ROWS // 2, ROWS))
            self.copy(6).start()

        def total(self):
            a, t = self.a, self.t
            out = part[a, t, self.chip(0, 0), c].astype(F32)
            for i, slot in ((5, 4), (6, 5), (7, 6)):
                self.copy(i).wait_recv()
                out = out + far_in[a, t, slot].astype(F32)
            return out

        def sent(self):
            for i in range(8):
                self.copy(i).wait_send()

    m = [Scatter(0, t) for t in range(3)]
    g = [Scatter(1, t) for t in range(3)]

    away = (4, 3, 3, 2, 2, 1, 1)

    def chunk_o(k):
        return lax.rem(lax.div(k, 2) + 4 - lead, 4) * 2 + lax.rem(k, 2)

    def chunk_i(k):
        return k

    class Chain:
        def __init__(self, grad, recv, send_sem, recv_sem, half, chunk):
            self.grad, self.recv, self.send_sem, self.recv_sem = grad, recv, send_sem, recv_sem
            self.half, self.chunk = half, chunk

        def place(self, i, way, distance):
            part_of = way if i % 2 == 0 else 1 - way
            k = self.chunk(ring(z, distance * (1 - 2 * way), 8))
            return at(k * 2 + part_of, self.half)

        def copy(self, i, way):
            return remote(
                self.grad.at[self.place(i, way, away[i]), :], self.recv.at[i, way],
                self.send_sem.at[i, way], self.recv_sem.at[i, way], (up, down)[way],
            )

        def arrive(self, i, way):
            self.copy(i, way).wait_recv()
            here = self.place(i, way, away[i] - 1)
            self.grad[here, :] = self.grad[here, :] + self.recv[i, way]

        def start(self):
            for i in range(2):
                for way in range(2):
                    self.copy(i, way).start()

        def step(self, i):
            for way in range(2):
                self.arrive(i - 2, way)
                self.copy(i, way).start()

        def end(self):
            for i in (5, 6):
                for way in range(2):
                    self.arrive(i, way)

        def sent(self):
            for i in range(7):
                for way in range(2):
                    self.copy(i, way).wait_send()

    zo = Chain(grad_o, recv_o, zo_s, zo_r, HALF, chunk_o)
    zq = Chain(grad_i.at[0], recv_i.at[0], zi_s.at[0], zi_r.at[0], HALF // 2, chunk_i)
    zk = Chain(grad_i.at[1], recv_i.at[1], zi_s.at[1], zi_r.at[1], HALF // 2, chunk_i)

    def grad_out(t):
        first, size = d_parts[t]
        cols = slice(first, first + size)
        grad_o[cols, :] = dot(ctx_t[...], fd[:, cols]).astype(BF).T

    def back_out(t):
        first, size = d_parts[t]
        cols = slice(first, first + size)
        term = dot(fd[:, cols], wout[:, cols], ABT)
        if t == 0:
            acc[:, :QC] = term
        elif t == 1:
            acc[:, :QC] += term
        else:
            dctx[...] = (acc[:, :QC] + term).astype(BF)

    pltpu.make_async_copy(wo, wout, in_sem.at[6]).wait()
    d[2].step2()
    d[0].step4()
    d[1].step3()
    for t in range(3):
        m[t].start(dot(ctx[...], wout[:, third(t)]))
    d[0].end()
    grad_out(0)
    zo.start()
    back_out(0)
    d[1].step4()
    d[2].step3()
    d[1].end()
    grad_out(1)
    back_out(1)
    from_next(0).wait_recv()
    from_sibling(0).start()
    zo.step(2)
    d[2].step4()
    d[2].end()
    back_out(2)

    def pair_copy(i):
        cols = (pl.ds(0, 128), pl.ds(128, 128), pl.ds(256, 256))[i]
        return remote(
            dqkv.at[:, cols], dqkv_x.at[:, cols], y_s.at[2 + i], y_r.at[2 + i], other_y
        )

    acc[...] = jnp.zeros_like(acc)

    def attend_back(h):
        for lo, hi in blocks:
            heads = slice(h * HEAD, (h + 1) * HEAD)
            d_ctx = dctx[lo:hi, heads]
            p = probs[h, lo:hi, :hi]
            d_p = dot(d_ctx, qkv[:hi, 384:512], ABT)
            inner = jnp.sum(p * d_p, axis=-1, keepdims=True)
            d_s = (slope[h, lo:hi, :hi] * (d_p - inner)).astype(BF)
            dqkv[lo:hi, heads] = dot(d_s, qkv[:hi, 256:384]).astype(BF)
            acc[:hi, 256:384] += dot(d_s, qkv[lo:hi, heads], ATB)
            acc[:hi, 384:512] += dot(p.astype(BF), d_ctx, ATB)
        pair_copy(h).start()

    attend_back(0)
    attend_back(1)
    dqkv[:, 256:512] = acc[:, 256:512].astype(BF)
    pair_copy(2).start()
    for t in range(3):
        m[t].spread()
    grad_out(2)
    zo.step(3)
    from_next(1).wait_recv()
    from_sibling(1).start()

    def back_in(t):
        g[t].start(dot(dqkv[...], w[third(t), :], ABT))

    back_in(0)
    back_in(1)
    m[0].middle()
    zo.step(4)
    back_in(2)
    m[1].middle()
    m[2].middle()
    g[0].spread()
    g[1].spread()
    zo.step(5)
    m[0].late()
    m[1].late()
    g[2].spread()
    zo.step(6)
    m[2].late()
    for i in range(2):
        from_sibling(i).wait_recv()
    for i in range(3):
        pair_copy(i).wait_recv()

    own_t = dqkv[...].T
    pair_t = dqkv_x[...].T
    for i in range(2):
        rows = slice(i * QUARTER, (i + 1) * QUARTER)
        own = slice(SIDE + i * QUARTER, SIDE + (i + 1) * QUARTER)
        term = (dot(own_t, fn[:, own]) + dot(pair_t, fx[:, rows])).astype(BF)
        grad_i[0, rows, :] = term[:256].T
        grad_i[1, rows, :] = term[256:].T
    zq.start()
    zk.start()

    def keep(h):
        return at(chunk_o(z) * 2 + h, HALF)

    g[0].middle()
    zo.end()
    y_copy = remote(grad_o.at[keep(1 - yh), :], recv_y, y_s.at[0], y_r.at[0], other_y)
    y_copy.start()
    zq.step(2)
    zk.step(2)
    g[1].middle()
    for t in range(3):
        mix_sum[:, third(t)] = m[t].total()
    for j in range(4):
        mixed[:, quarter(j)] = (
            tok[:, quarter(j)].astype(F32) + mix_sum[:, j * QUARTER : (j + 1) * QUARTER]
        ).astype(BF)
    mixed_out = pltpu.make_async_copy(mixed, mixed_o, out_sem.at[0])
    mixed_out.start()
    g[0].late()
    zq.step(3)
    zk.step(3)
    g[2].middle()
    g[1].late()
    zq.step(4)
    zk.step(4)
    for gather in n + d:
        gather.sent()
    g[2].late()
    zq.step(5)
    zk.step(5)
    y_copy.wait()
    dwo[...] = grad_o[keep(yh), :].astype(F32) + recv_y[...].astype(F32)
    dwo_out = pltpu.make_async_copy(dwo, dwo_o, out_sem.at[5])
    dwo_out.start()
    for stream in m:
        stream.sent()
    zo.sent()
    zq.step(6)
    zk.step(6)

    sums = [g[t].total() for t in range(3)]
    summed = jnp.concatenate(sums, axis=1)
    first = jnp.where(yh == 0, summed[:, SIDE:], summed[:, :SIDE])
    second = jnp.where(yh == 0, summed[:, :SIDE], summed[:, SIDE:])
    d_normed = jnp.concatenate(
        [
            side[:, k * HALF : (k + 1) * HALF]
            for k in range(8)
            for side in (first, second)
        ],
        axis=1,
    )
    upstream = gain[...] * d_normed
    values = tok[...].astype(F32)
    scale = lax.rsqrt(jnp.mean(values * values, axis=-1, keepdims=True) + 1e-06)
    back_norm = scale * upstream - values * (scale * scale * scale) * jnp.mean(
        upstream * values, axis=-1, keepdims=True
    )
    dtok[...] = (dm[...].astype(F32) + back_norm).astype(BF)
    dtok_out = pltpu.make_async_copy(dtok, dtok_o, out_sem.at[1])
    dtok_out.start()

    zq.end()
    dwq[...] = grad_i[0, at(z, HALF), :].astype(F32)
    dwq_out = pltpu.make_async_copy(dwq, dwq_o, out_sem.at[2])
    dwq_out.start()
    zk.end()
    dwk[...] = grad_i[1, at(z, HALF), :HEAD].astype(F32)
    dwv[...] = grad_i[1, at(z, HALF), HEAD:].astype(F32)
    dwk_out = pltpu.make_async_copy(dwk, dwk_o, out_sem.at[3])
    dwk_out.start()
    dwv_out = pltpu.make_async_copy(dwv, dwv_o, out_sem.at[4])
    dwv_out.start()

    for stream in g:
        stream.sent()
    zq.sent()
    zk.sent()
    for i in range(2):
        from_next(i).wait_send()
        from_sibling(i).wait_send()
    for i in range(3):
        pair_copy(i).wait_send()
    for copy in (mixed_out, dtok_out, dwq_out, dwk_out, dwv_out, dwo_out):
        copy.wait()


def hand_out(*refs):
    sources, results, held, sem = refs[:6], refs[6:12], refs[12:18], refs[18]
    loads = [
        pltpu.make_async_copy(source, ref, sem.at[0, i])
        for i, (source, ref) in enumerate(zip(sources, held))
    ]
    stores = [
        pltpu.make_async_copy(ref, result, sem.at[1, i])
        for i, (ref, result) in enumerate(zip(held, results))
    ]
    for load in loads:
        load.start()
    for load, store in zip(loads, stores):
        load.wait()
        store.start()
    for store in stores:
        store.wait()


def on_device(tokens, norm_gain, w_query, w_key, w_value, w_output, d_mixed):
    hbm = pl.BlockSpec(memory_space=pltpu.HBM)
    dma = pltpu.SemaphoreType.DMA
    results = (
        jax.ShapeDtypeStruct((ROWS, D), BF),
        jax.ShapeDtypeStruct((ROWS, D), BF),
        jax.ShapeDtypeStruct((HALF, QC), F32),
        jax.ShapeDtypeStruct((HALF, HEAD), F32),
        jax.ShapeDtypeStruct((HALF, HEAD), F32),
        jax.ShapeDtypeStruct((HALF, QC), F32),
    )
    made = pl.pallas_call(
        kernel,
        out_shape=results,
        in_specs=[hbm] * 7,
        out_specs=(hbm,) * 6,
        scratch_shapes=[
            pltpu.VMEM((ROWS, D), BF),
            pltpu.VMEM((D,), F32),
            pltpu.VMEM((ROWS, D), BF),
            *(pltpu.VMEM(r.shape, r.dtype) for r in results),
            pltpu.VMEM((ROWS, D), F32),
            pltpu.VMEM((SEQ, D), BF),
            pltpu.VMEM((SEQ, D), BF),
            pltpu.VMEM((SEQ, SIDE), BF),
            pltpu.VMEM((D, 512), BF),
            pltpu.VMEM((QC, D), BF),
            pltpu.VMEM((SEQ, 512), BF),
            pltpu.VMEM((SEQ, QC), BF),
            pltpu.VMEM((QC, SEQ), BF),
            pltpu.VMEM((SEQ, QC), BF),
            pltpu.VMEM((SEQ, 512), BF),
            pltpu.VMEM((SEQ, 512), BF),
            pltpu.VMEM((SEQ, 512), F32),
            pltpu.VMEM((2, SEQ, SEQ), F32),
            pltpu.VMEM((2, SEQ, SEQ), F32),
            pltpu.VMEM((D, QC), BF),
            pltpu.VMEM((2, SIDE, QC), BF),
            pltpu.VMEM((7, 2, HALF, QC), BF),
            pltpu.VMEM((2, 7, 2, HALF // 2, QC), BF),
            pltpu.VMEM((HALF, QC), BF),
            pltpu.VMEM((2, 3, 8, 2, ROWS, THIRD), BF),
            pltpu.VMEM((2, 3, 8, ROWS, THIRD), BF),
            pltpu.VMEM((2, 3, 7, ROWS, THIRD), BF),
            dma((7,)),
            dma((6,)),
            dma((6, 16)),
            dma((6, 16)),
            dma((4,)),
            dma((4,)),
            dma((7, 2)),
            dma((7, 2)),
            dma((2, 7, 2)),
            dma((2, 7, 2)),
            dma((5,)),
            dma((5,)),
            dma((2, 3)),
            dma((2, 3)),
            dma((2, 3, 8)),
            dma((2, 3, 8)),
        ],
        compiler_params=pltpu.CompilerParams(
            collective_id=0, has_side_effects=True, vmem_limit_bytes=64 * 2**20 - 2**17
        ),
        cost_estimate=pl.CostEstimate(
            flops=12 * 10**9, bytes_accessed=10**7, transcendentals=10**6
        ),
    )(tokens, norm_gain, w_query, w_key, w_value, w_output, d_mixed)
    mixed, d_tokens, dw_query, dw_key, dw_value, dw_out_t = pl.pallas_call(
        hand_out,
        out_shape=results,
        in_specs=[hbm] * 6,
        out_specs=(hbm,) * 6,
        scratch_shapes=[pltpu.VMEM(r.shape, r.dtype) for r in results] + [dma((2, 6))],
    )(*made)
    return (mixed, d_tokens, dw_query, dw_key, dw_value, dw_out_t.T)


def solution(mesh):
    return jax.shard_map(
        on_device,
        mesh=mesh,
        in_specs=(
            P(("dp", "tensor"), None),
            P(),
            P(None, "tensor"),
            P(None, "tensor"),
            P(None, "tensor"),
            P("tensor", None),
            P(("dp", "tensor"), None),
        ),
        out_specs=(
            P(("dp", "tensor"), None),
            P(("dp", "tensor"), None),
            P("dp", "tensor"),
            P("dp", "tensor"),
            P("dp", "tensor"),
            P("tensor", "dp"),
        ),
        check_vma=False,
    )
```

time: 1100 us -> 109 us (0.10)
  waiting for transfers between devices: 997 us -> 0 us
  Pallas kernels: 0 us -> 108 us
  matrix products: 59.6 us -> 0 us
  other arithmetic: 13.7 us -> 0 us
  between operations: 14.5 us -> 0.8 us
    reduce_scatter x5 -> x0, waiting for transfers between devices: 705 us -> none  [the longest x1 211 us: on_device(): lax.psum_scatter(inner_rows(normed, d_query).astype(jnp.bfloat16), 'dp',...]
    unnamed x9 -> x0, waiting for transfers between devices: 214 us -> none
    pallas_call x0 -> x2, Pallas kernels: none -> 108 us  [the longest x1 106 us: on_device(): pl.pallas_call(kernel, out_shape=results, in_specs=[hbm] * 7, out_specs=(...]
    all_gather x2 -> x0, waiting for transfers between devices: 78 us -> none  [the longest x1 44.4 us: on_device(): lax.all_gather(norm_rows(tokens, norm_gain), 'tensor', axis=0, tiled=True)]
    dot_general x18 -> x0, matrix products: 59.6 us -> none  [the longest x4 20.2 us: right_trans(): lax.dot_general(left, right, (((1,), (1,)), ((), ())), preferred_element_...]
  transfers between devices with their start and end apart: 8 -> 0, of which waited for: 8 -> 0; matrix products, arithmetic and copies ran while one was open for 6% -> 0% of each run, Pallas kernels for 0% -> 0%
where the time goes in v3:
time: 109 us
  Pallas kernels  108 us (99%)
    pallas_call x1, Pallas kernels, on_device(): pl.pallas_call(kernel, out_shape=results, in_specs=[hbm] * 7, out_specs=(...  106 us

profile of v3, /device:TPU:1, one launch (start us, length us, event | category | flops | bytes accessed | tf_op | source)
XLA Modules:
  0.0 108.7 jit_solution(13371401619011932835)
XLA Ops:
  0.6 105.7 %shard_map.118 = (bf16[32,4608]{1,0:T(8,128)(2,1)}, bf16[32,4608]{1,0:T(8,128)(2,1)}, f32[288,256]{1,0:T(8,128)}, f32[288,128]{1,0:T(8,128)}, f32[288,128]{1,0:T(8,128)}, /*index=5*/f32[288,256]{1,0:T(8,128)}) custom-call(bf16[32,4608]{1,0:T(8,128)(2,1)} %tok_h.1, f32[4608]{0:T(1024)} %gain_h.1, bf16[4608,256]{1,0:T(8,128)(2,1)} %wq.1, ...), custom_call_target="tpu_custom_call" | custom-call | flops 12000000000 | bytes 10000000 | tf_op jit(solution)/shard_map/pallas_call | solution.py:627
  106.3 2.2 %shard_map.119 = (bf16[32,4608]{1,0:T(8,128)(2,1)}, bf16[32,4608]{1,0:T(8,128)(2,1)}, f32[288,256]{1,0:T(8,128)}, f32[288,128]{1,0:T(8,128)}, f32[288,128]{1,0:T(8,128)}, /*index=5*/f32[288,256]{1,0:T(8,128)}) custom-call(bf16[32,4608]{1,0:T(8,128)(2,1)} %get-tuple-element.18.refs_0_, bf16[32,4608]{1,0:T(8,128)(2,1)} %get-tuple-element.19.refs_1_, ...), custom_call_target="tpu_custom_call" | custom-call | tf_op jit(solution)/shard_map/pallas_call | solution.py:684

commit v4 on v3

--- a/solution.py
+++ b/solution.py
@@ -431,14 +431,17 @@
     back_out(0)
     d[1].step4()
     d[2].step3()
+    m[0].spread()
     d[1].end()
     grad_out(1)
     back_out(1)
-    from_next(0).wait_recv()
-    from_sibling(0).start()
+    m[1].spread()
     zo.step(2)
     d[2].step4()
+    m[2].spread()
     d[2].end()
+    grad_out(2)
+    zo.step(3)
     back_out(2)
 
     def pair_copy(i):
@@ -463,48 +466,53 @@
         pair_copy(h).start()
 
     attend_back(0)
+    zo.step(4)
     attend_back(1)
     dqkv[:, 256:512] = acc[:, 256:512].astype(BF)
     pair_copy(2).start()
-    for t in range(3):
-        m[t].spread()
-    grad_out(2)
-    zo.step(3)
+    from_next(0).wait_recv()
+    from_sibling(0).start()
+
+    def back_in(t):
+        g[t].start(dot(dqkv[...], w[third(t), :], ABT))
+
+    back_in(0)
+    zo.step(5)
+    back_in(1)
+    m[0].middle()
+    back_in(2)
+    zo.step(6)
     from_next(1).wait_recv()
     from_sibling(1).start()
-
-    def back_in(t):
-        g[t].start(dot(dqkv[...], w[third(t), :], ABT))
-
-    back_in(0)
-    back_in(1)
-    m[0].middle()
-    zo.step(4)
-    back_in(2)
     m[1].middle()
     m[2].middle()
     g[0].spread()
+    m[0].late()
     g[1].spread()
-    zo.step(5)
-    m[0].late()
-    m[1].late()
-    g[2].spread()
-    zo.step(6)
-    m[2].late()
     for i in range(2):
         from_sibling(i).wait_recv()
-    for i in range(3):
-        pair_copy(i).wait_recv()
-
-    own_t = dqkv[...].T
-    pair_t = dqkv_x[...].T
-    for i in range(2):
-        rows = slice(i * QUARTER, (i + 1) * QUARTER)
-        own = slice(SIDE + i * QUARTER, SIDE + (i + 1) * QUARTER)
-        term = (dot(own_t, fn[:, own]) + dot(pair_t, fx[:, rows])).astype(BF)
-        grad_i[0, rows, :] = term[:256].T
-        grad_i[1, rows, :] = term[256:].T
+
+    def grad_in(which):
+        cols = slice(which * QC, (which + 1) * QC)
+        own_t = dqkv[:, cols].T
+        pair_t = dqkv_x[:, cols].T
+        for i in range(2):
+            rows = slice(i * QUARTER, (i + 1) * QUARTER)
+            own = slice(SIDE + i * QUARTER, SIDE + (i + 1) * QUARTER)
+            term = dot(own_t, fn[:, own]) + dot(pair_t, fx[:, rows])
+            grad_i[which, rows, :] = term.astype(BF).T
+
+    pair_copy(0).wait_recv()
+    pair_copy(1).wait_recv()
+    grad_in(0)
     zq.start()
+    g[2].spread()
+    m[1].late()
+    m[2].late()
+    zq.step(2)
+    zq.step(3)
+    pair_copy(2).wait_recv()
+    grad_in(1)
     zk.start()
 
     def keep(h):
@@ -514,9 +522,11 @@
     zo.end()
     y_copy = remote(grad_o.at[keep(1 - yh), :], recv_y, y_s.at[0], y_r.at[0], other_y)
     y_copy.start()
-    zq.step(2)
+    g[1].middle()
+    zq.step(4)
     zk.step(2)
-    g[1].middle()
+    g[2].middle()
+    zq.step(5)
     for t in range(3):
         mix_sum[:, third(t)] = m[t].total()
     for j in range(4):
@@ -525,27 +535,27 @@
         ).astype(BF)
     mixed_out = pltpu.make_async_copy(mixed, mixed_o, out_sem.at[0])
     mixed_out.start()
+    zk.step(3)
     g[0].late()
-    zq.step(3)
-    zk.step(3)
-    g[2].middle()
+    zq.step(6)
+    zk.step(4)
     g[1].late()
-    zq.step(4)
-    zk.step(4)
-    for gather in n + d:
-        gather.sent()
     g[2].late()
-    zq.step(5)
     zk.step(5)
     y_copy.wait()
     dwo[...] = grad_o[keep(yh), :].astype(F32) + recv_y[...].astype(F32)
     dwo_out = pltpu.make_async_copy(dwo, dwo_o, out_sem.at[5])
     dwo_out.start()
+    for gather in n + d:
+        gather.sent()
     for stream in m:
         stream.sent()
     zo.sent()
-    zq.step(6)
     zk.step(6)
+    zq.end()
+    dwq[...] = grad_i[0, at(z, HALF), :].astype(F32)
+    dwq_out = pltpu.make_async_copy(dwq, dwq_o, out_sem.at[2])
+    dwq_out.start()
 
     sums = [g[t].total() for t in range(3)]
     summed = jnp.concatenate(sums, axis=1)
@@ -569,10 +579,6 @@
     dtok_out = pltpu.make_async_copy(dtok, dtok_o, out_sem.at[1])
     dtok_out.start()
 
-    zq.end()
-    dwq[...] = grad_i[0, at(z, HALF), :].astype(F32)
-    dwq_out = pltpu.make_async_copy(dwq, dwq_o, out_sem.at[2])
-    dwq_out.start()
     zk.end()
     dwk[...] = grad_i[1, at(z, HALF), :HEAD].astype(F32)
     dwv[...] = grad_i[1, at(z, HALF), HEAD:].astype(F32)

time: 109 us -> 99.8 us (0.916)
  Pallas kernels: 108 us -> 98.8 us
    pallas_call x1, Pallas kernels: 106 us -> 96.7 us  [on_device(): pl.pallas_call(kernel, out_shape=results, in_specs=[hbm] * 7, out_specs=(...]
where the time goes in v4:
time: 99.8 us; the launch traced here: 99.7 us
  Pallas kernels  98.8 us (99%)
    pallas_call x1, Pallas kernels, on_device(): pl.pallas_call(kernel, out_shape=results, in_specs=[hbm] * 7, out_specs=(...  96.7 us
    pallas_call x1, Pallas kernels, on_device(): pl.pallas_call(hand_out, out_shape=results, in_specs=[hbm] * 6, out_specs...  2.17 us

profile of v4, /device:TPU:1, one launch (start us, length us, event | category | flops | bytes accessed | tf_op | source)
XLA Modules:
  0.0 99.7 jit_solution(4739533208565733854)
XLA Ops:
  0.6 96.7 %shard_map.118 = (bf16[32,4608]{1,0:T(8,128)(2,1)}, bf16[32,4608]{1,0:T(8,128)(2,1)}, f32[288,256]{1,0:T(8,128)}, f32[288,128]{1,0:T(8,128)}, f32[288,128]{1,0:T(8,128)}, /*index=5*/f32[288,256]{1,0:T(8,128)}) custom-call(bf16[32,4608]{1,0:T(8,128)(2,1)} %tok_h.1, f32[4608]{0:T(1024)} %gain_h.1, bf16[4608,256]{1,0:T(8,128)(2,1)} %wq.1, ...), custom_call_target="tpu_custom_call" | custom-call | flops 12000000000 | bytes 10000000 | tf_op jit(solution)/shard_map/pallas_call | solution.py:633
  97.3 2.2 %shard_map.119 = (bf16[32,4608]{1,0:T(8,128)(2,1)}, bf16[32,4608]{1,0:T(8,128)(2,1)}, f32[288,256]{1,0:T(8,128)}, f32[288,128]{1,0:T(8,128)}, f32[288,128]{1,0:T(8,128)}, /*index=5*/f32[288,256]{1,0:T(8,128)}) custom-call(bf16[32,4608]{1,0:T(8,128)(2,1)} %get-tuple-element.18.refs_0_, bf16[32,4608]{1,0:T(8,128)(2,1)} %get-tuple-element.19.refs_1_, ...), custom_call_target="tpu_custom_call" | custom-call | tf_op jit(solution)/shard_map/pallas_call | solution.py:690

commit v5 on v4

--- a/solution.py
+++ b/solution.py
@@ -102,102 +102,6 @@
     dm_in.wait()
     for j in range(4):
         fd[mine, j * QUARTER : (j + 1) * QUARTER] = dm[:, quarter(j)]
-    pl.semaphore_wait(barrier, len(peers))
-
-    def block(dx, dy, core):
-        return (yl if dy == 0 else 1 - yl) * 8 + ring(x, dx, 4) * 2 + core
-
-    class Gather:
-        order = ((0, 0), (-1, 0), (1, 0), (0, 1), (2, 0), (-1, 1), (1, 1), (2, 1))
-
-        def __init__(self, full, a, first_column, columns):
-            self.full, self.a = full, a
-            self.columns = pl.ds(first_column, columns)
-
-        def copy(self, i, rows, to):
-            ref = self.full.at[rows, self.columns]
-            return remote(ref, ref, ag_s.at[self.a, i], ag_r.at[self.a, i], to)
-
-        def whole(self, dx, dy, core=c):
-            return at(block(dx, dy, core), ROWS)
-
-        def piece(self, dx, half):
-            return at(block(dx, 0, c) * 2 + half, ROWS // 2)
-
-        def to_sibling(self, i):
-            self.copy(8 + i, self.whole(*self.order[i]), sibling).start()
-
-        def step1(self):
-            self.copy(0, self.whole(0, 0), right).start()
-            self.copy(1, self.whole(0, 0), left).start()
-            self.copy(2, self.whole(0, 0), across).start()
-            self.to_sibling(0)
-
-        def step2(self):
-            self.copy(0, self.whole(-1, 0), right).wait_recv()
-            self.copy(3, self.piece(-1, 0), right).start()
-            self.copy(1, self.whole(1, 0), left).wait_recv()
-            self.copy(4, self.piece(1, 1), left).start()
-            self.copy(2, self.whole(0, 1), across).wait_recv()
-            self.copy(5, self.whole(0, 1), right).start()
-            self.copy(6, self.whole(0, 1), left).start()
-            for i in (1, 2, 3):
-                self.to_sibling(i)
-
-        def step3(self):
-            self.copy(3, self.piece(2, 0), right).wait_recv()
-            self.copy(4, self.piece(2, 1), left).wait_recv()
-            self.copy(7, self.whole(2, 0), across).start()
-            self.to_sibling(4)
-
-        def step4(self):
-            self.copy(5, self.whole(-1, 1), right).wait_recv()
-            self.to_sibling(5)
-            self.copy(6, self.whole(1, 1), left).wait_recv()
-            self.to_sibling(6)
-            self.copy(7, self.whole(2, 1), across).wait_recv()
-            self.to_sibling(7)
-
-        def end(self):
-            for i in range(8):
-                self.copy(8 + i, self.whole(*self.order[i], 1 - c), sibling).wait_recv()
-
-        def sent(self):
-            for i, to in ((0, right), (1, left), (2, across), (5, right), (6, left), (7, across)):
-                self.copy(i, self.whole(0, 0), to).wait_send()
-            self.copy(3, self.piece(0, 0), right).wait_send()
-            self.copy(4, self.piece(0, 0), left).wait_send()
-            for i in range(8):
-                self.copy(8 + i, self.whole(0, 0), sibling).wait_send()
-
-    n = [Gather(fn, t, t * THIRD, THIRD) for t in range(3)]
-    d_parts = ((0, 2 * QUARTER), (2 * QUARTER, QUARTER), (3 * QUARTER, QUARTER))
-    d = [Gather(fd, 3 + t, *d_parts[t]) for t in range(3)]
-
-    pieces = ((0, THIRD), (THIRD, SIDE - THIRD))
-
-    def from_next(i):
-        ref = (at(c, SEQ // 2), pl.ds(*pieces[i]))
-        return remote(fn.at[ref], fx.at[ref], hi_s.at[i], hi_r.at[i], next_y)
-
-    def from_sibling(i):
-        ref = fx.at[at(c, SEQ // 2), pl.ds(*pieces[i])]
-        return remote(ref, ref, hi_s.at[2 + i], hi_r.at[2 + i], sibling)
-
-    def third(t):
-        return slice(t * THIRD, (t + 1) * THIRD)
-
-    def project(t):
-        term = dot(fn[:, third(t)], w[third(t), :])
-        if t == 0:
-            acc[...] = term
-        elif t == 1:
-            acc[...] += term
-        else:
-            qkv[...] = (acc[...] + term).astype(BF)
-
-    n[0].step1()
-    n[1].step1()
 
     columns = (pl.ds(0, 256), pl.ds(256, 128), pl.ds(384, 128))
     for i, weight in enumerate((wq, wk, wv)):
@@ -212,6 +116,102 @@
         pltpu.make_async_copy(
             wo.at[:, quarter(j)], wout.at[:, pl.ds(j * QUARTER, QUARTER)], in_sem.at[6]
         ).start()
+    pl.semaphore_wait(barrier, len(peers))
+
+    def block(dx, dy, core):
+        return (yl if dy == 0 else 1 - yl) * 8 + ring(x, dx, 4) * 2 + core
+
+    class Gather:
+        order = ((0, 0), (-1, 0), (1, 0), (0, 1), (2, 0), (-1, 1), (1, 1), (2, 1))
+
+        def __init__(self, full, a, first_column, columns):
+            self.full, self.a = full, a
+            self.columns = pl.ds(first_column, columns)
+
+        def copy(self, i, rows, to):
+            ref = self.full.at[rows, self.columns]
+            return remote(ref, ref, ag_s.at[self.a, i], ag_r.at[self.a, i], to)
+
+        def whole(self, dx, dy, core=c):
+            return at(block(dx, dy, core), ROWS)
+
+        def piece(self, dx, half):
+            return at(block(dx, 0, c) * 2 + half, ROWS // 2)
+
+        def to_sibling(self, i):
+            self.copy(8 + i, self.whole(*self.order[i]), sibling).start()
+
+        def step1(self):
+            self.copy(0, self.whole(0, 0), right).start()
+            self.copy(1, self.whole(0, 0), left).start()
+            self.copy(2, self.whole(0, 0), across).start()
+            self.to_sibling(0)
+
+        def step2(self):
+            self.copy(0, self.whole(-1, 0), right).wait_recv()
+            self.copy(3, self.piece(-1, 0), right).start()
+            self.copy(1, self.whole(1, 0), left).wait_recv()
+            self.copy(4, self.piece(1, 1), left).start()
+            self.copy(2, self.whole(0, 1), across).wait_recv()
+            self.copy(5, self.whole(0, 1), right).start()
+            self.copy(6, self.whole(0, 1), left).start()
+            for i in (1, 2, 3):
+                self.to_sibling(i)
+
+        def step3(self):
+            self.copy(3, self.piece(2, 0), right).wait_recv()
+            self.copy(4, self.piece(2, 1), left).wait_recv()
+            self.copy(7, self.whole(2, 0), across).start()
+            self.to_sibling(4)
+
+        def step4(self):
+            self.copy(5, self.whole(-1, 1), right).wait_recv()
+            self.to_sibling(5)
+            self.copy(6, self.whole(1, 1), left).wait_recv()
+            self.to_sibling(6)
+            self.copy(7, self.whole(2, 1), across).wait_recv()
+            self.to_sibling(7)
+
+        def end(self):
+            for i in range(8):
+                self.copy(8 + i, self.whole(*self.order[i], 1 - c), sibling).wait_recv()
+
+        def sent(self):
+            for i, to in ((0, right), (1, left), (2, across), (5, right), (6, left), (7, across)):
+                self.copy(i, self.whole(0, 0), to).wait_send()
+            self.copy(3, self.piece(0, 0), right).wait_send()
+            self.copy(4, self.piece(0, 0), left).wait_send()
+            for i in range(8):
+                self.copy(8 + i, self.whole(0, 0), sibling).wait_send()
+
+    n = [Gather(fn, t, t * THIRD, THIRD) for t in range(3)]
+    d_parts = ((0, 2 * QUARTER), (2 * QUARTER, QUARTER), (3 * QUARTER, QUARTER))
+    d = [Gather(fd, 3 + t, *d_parts[t]) for t in range(3)]
+
+    pieces = ((0, THIRD), (THIRD, SIDE - THIRD))
+
+    def from_next(i):
+        ref = (at(c, SEQ // 2), pl.ds(*pieces[i]))
+        return remote(fn.at[ref], fx.at[ref], hi_s.at[i], hi_r.at[i], next_y)
+
+    def from_sibling(i):
+        ref = fx.at[at(c, SEQ // 2), pl.ds(*pieces[i])]
+        return remote(ref, ref, hi_s.at[2 + i], hi_r.at[2 + i], sibling)
+
+    def third(t):
+        return slice(t * THIRD, (t + 1) * THIRD)
+
+    def project(t):
+        term = dot(fn[:, third(t)], w[third(t), :])
+        if t == 0:
+            acc[...] = term
+        elif t == 1:
+            acc[...] += term
+        else:
+            qkv[...] = (acc[...] + term).astype(BF)
+
+    n[0].step1()
+    n[1].step1()
 
     n[0].step2()
     n[2].step1()
@@ -485,10 +485,10 @@
     from_next(1).wait_recv()
     from_sibling(1).start()
     m[1].middle()
+    g[0].spread()
     m[2].middle()
-    g[0].spread()
-    m[0].late()
     g[1].spread()
+    g[2].spread()
     for i in range(2):
         from_sibling(i).wait_recv()
 
@@ -506,27 +506,31 @@
     pair_copy(1).wait_recv()
     grad_in(0)
     zq.start()
-    g[2].spread()
+    m[0].late()
     m[1].late()
+    zq.step(2)
     m[2].late()
-    zq.step(2)
     zq.step(3)
     pair_copy(2).wait_recv()
     grad_in(1)
     zk.start()
+    zq.step(4)
 
     def keep(h):
         return at(chunk_o(z) * 2 + h, HALF)
 
+    zo.end()
+    zk.step(2)
     g[0].middle()
-    zo.end()
+    zq.step(5)
+    g[1].middle()
+    zk.step(3)
+    g[2].middle()
+    zq.step(6)
     y_copy = remote(grad_o.at[keep(1 - yh), :], recv_y, y_s.at[0], y_r.at[0], other_y)
     y_copy.start()
-    g[1].middle()
-    zq.step(4)
-    zk.step(2)
-    g[2].middle()
-    zq.step(5)
+    g[0].late()
+    zk.step(4)
     for t in range(3):
         mix_sum[:, third(t)] = m[t].total()
     for j in range(4):
@@ -535,23 +539,19 @@
         ).astype(BF)
     mixed_out = pltpu.make_async_copy(mixed, mixed_o, out_sem.at[0])
     mixed_out.start()
-    zk.step(3)
-    g[0].late()
-    zq.step(6)
-    zk.step(4)
     g[1].late()
+    zk.step(5)
     g[2].late()
-    zk.step(5)
-    y_copy.wait()
-    dwo[...] = grad_o[keep(yh), :].astype(F32) + recv_y[...].astype(F32)
-    dwo_out = pltpu.make_async_copy(dwo, dwo_o, out_sem.at[5])
-    dwo_out.start()
     for gather in n + d:
         gather.sent()
     for stream in m:
         stream.sent()
     zo.sent()
     zk.step(6)
+    y_copy.wait()
+    dwo[...] = grad_o[keep(yh), :].astype(F32) + recv_y[...].astype(F32)
+    dwo_out = pltpu.make_async_copy(dwo, dwo_o, out_sem.at[5])
+    dwo_out.start()
     zq.end()
     dwq[...] = grad_i[0, at(z, HALF), :].astype(F32)
     dwq_out = pltpu.make_async_copy(dwq, dwq_o, out_sem.at[2])

time: 99.8 us -> 98.2 us (0.984)
  Pallas kernels: 98.8 us -> 97 us
    pallas_call x1, Pallas kernels: 96.7 us -> 94.8 us  [on_device(): pl.pallas_call(kernel, out_shape=results, in_specs=[hbm] * 7, out_specs=(...]
where the time goes in v5:
time: 98.2 us; the launch traced here: 97.8 us
  Pallas kernels  97 us (99%)
    pallas_call x1, Pallas kernels, on_device(): pl.pallas_call(kernel, out_shape=results, in_specs=[hbm] * 7, out_specs=(...  94.8 us
    pallas_call x1, Pallas kernels, on_device(): pl.pallas_call(hand_out, out_shape=results, in_specs=[hbm] * 6, out_specs...  2.17 us

profile of v5, /device:TPU:1, one launch (start us, length us, event | category | flops | bytes accessed | tf_op | source)
XLA Modules:
  0.0 97.8 jit_solution(2854989277443281920)
XLA Ops:
  0.6 94.8 %shard_map.118 = (bf16[32,4608]{1,0:T(8,128)(2,1)}, bf16[32,4608]{1,0:T(8,128)(2,1)}, f32[288,256]{1,0:T(8,128)}, f32[288,128]{1,0:T(8,128)}, f32[288,128]{1,0:T(8,128)}, /*index=5*/f32[288,256]{1,0:T(8,128)}) custom-call(bf16[32,4608]{1,0:T(8,128)(2,1)} %tok_h.1, f32[4608]{0:T(1024)} %gain_h.1, bf16[4608,256]{1,0:T(8,128)(2,1)} %wq.1, ...), custom_call_target="tpu_custom_call" | custom-call | flops 12000000000 | bytes 10000000 | tf_op jit(solution)/shard_map/pallas_call | solution.py:633
  95.4 2.2 %shard_map.119 = (bf16[32,4608]{1,0:T(8,128)(2,1)}, bf16[32,4608]{1,0:T(8,128)(2,1)}, f32[288,256]{1,0:T(8,128)}, f32[288,128]{1,0:T(8,128)}, f32[288,128]{1,0:T(8,128)}, /*index=5*/f32[288,256]{1,0:T(8,128)}) custom-call(bf16[32,4608]{1,0:T(8,128)(2,1)} %get-tuple-element.18.refs_0_, bf16[32,4608]{1,0:T(8,128)(2,1)} %get-tuple-element.19.refs_1_, ...), custom_call_target="tpu_custom_call" | custom-call | tf_op jit(solution)/shard_map/pallas_call | solution.py:690

commit v6 on v5

--- a/solution.py
+++ b/solution.py
@@ -496,11 +496,8 @@
         cols = slice(which * QC, (which + 1) * QC)
         own_t = dqkv[:, cols].T
         pair_t = dqkv_x[:, cols].T
-        for i in range(2):
-            rows = slice(i * QUARTER, (i + 1) * QUARTER)
-            own = slice(SIDE + i * QUARTER, SIDE + (i + 1) * QUARTER)
-            term = dot(own_t, fn[:, own]) + dot(pair_t, fx[:, rows])
-            grad_i[which, rows, :] = term.astype(BF).T
+        term = dot(own_t, fn[:, SIDE:]) + dot(pair_t, fx[...])
+        grad_i[which] = term.astype(BF).T
 
     pair_copy(0).wait_recv()
     pair_copy(1).wait_recv()

time: 98.2 us -> 98.1 us (level)
  no operation moved by 1% of the time
where the time goes in v6:
time: 98.1 us; the launch traced here: 97.7 us
  Pallas kernels  96.9 us (99%)
    pallas_call x1, Pallas kernels, on_device(): pl.pallas_call(kernel, out_shape=results, in_specs=[hbm] * 7, out_specs=(...  94.7 us
    pallas_call x1, Pallas kernels, on_device(): pl.pallas_call(hand_out, out_shape=results, in_specs=[hbm] * 6, out_specs...  2.17 us

profile of v6, /device:TPU:1, one launch (start us, length us, event | category | flops | bytes accessed | tf_op | source)
XLA Modules:
  0.0 97.7 jit_solution(13779505869926604041)
XLA Ops:
  0.6 94.7 %shard_map.118 = (bf16[32,4608]{1,0:T(8,128)(2,1)}, bf16[32,4608]{1,0:T(8,128)(2,1)}, f32[288,256]{1,0:T(8,128)}, f32[288,128]{1,0:T(8,128)}, f32[288,128]{1,0:T(8,128)}, /*index=5*/f32[288,256]{1,0:T(8,128)}) custom-call(bf16[32,4608]{1,0:T(8,128)(2,1)} %tok_h.1, f32[4608]{0:T(1024)} %gain_h.1, bf16[4608,256]{1,0:T(8,128)(2,1)} %wq.1, ...), custom_call_target="tpu_custom_call" | custom-call | flops 12000000000 | bytes 10000000 | tf_op jit(solution)/shard_map/pallas_call | solution.py:630
  95.4 2.2 %shard_map.119 = (bf16[32,4608]{1,0:T(8,128)(2,1)}, bf16[32,4608]{1,0:T(8,128)(2,1)}, f32[288,256]{1,0:T(8,128)}, f32[288,128]{1,0:T(8,128)}, f32[288,128]{1,0:T(8,128)}, /*index=5*/f32[288,256]{1,0:T(8,128)}) custom-call(bf16[32,4608]{1,0:T(8,128)(2,1)} %get-tuple-element.18.refs_0_, bf16[32,4608]{1,0:T(8,128)(2,1)} %get-tuple-element.19.refs_1_, ...), custom_call_target="tpu_custom_call" | custom-call | tf_op jit(solution)/shard_map/pallas_call | solution.py:687
